TPU v7x, 32 devices: a whole 2x2x4 slice. The times are simulated.
32 devices in a mesh: region: 2 (over y), slab: 16 (over z, x, core).
Axes of the slice: x: 2, y: 2, z: 4, core: 2. Of those that a mesh axis runs over, the one named last changes fastest.
Arguments:
- magnetic: float32 [3, 256, 64, 256], P(None, 'slab', None, 'region'), may hold values from -6 to 6
- velocity: float32 [3, 256, 64, 256], P(None, 'slab', None, 'region'), may hold values from -12 to 12
- wall_response: float32 [256, 256, 256], P(('region', 'slab')), may hold values from -0.375 to 0.375
- mode_slots: int32 [256], replicated, may hold values from 0 to 255, each once
- wall_layers: int32 [256], P('region'), may hold values from 1 to 8
Outputs:
- magnetic_next: float32 [3, 256, 64, 256], P(None, 'slab', None, 'region')
- wall_flux: float32 [2, 256, 256], P(None, 'slab', 'region')
Inputs may be any that keep to these rules, and one draw needn't show every extreme that they name: `mode_slots`: each slot names a different mode.
All inputs are finite; a program needn't handle non-finite values.
Results may differ from a plain program's by a relative error of at most 0.00007.
Values sent between devices are 32-bit elements; how exact they have to be, the bound alone decides.
A program may use at most 128 MiB of HBM per device.

v0:
```python
import math

import jax
import jax.numpy as jnp
from jax import lax
from jax.sharding import PartitionSpec as P

LW = 8


TIME_STEP = 0.0003
DIFFUSIVITY = 0.001
RADIAL_STEP = 1.0 / 384.0
AXIAL_STEP = 1.0 / 768.0
HIGHEST = lax.Precision.HIGHEST


def with_halo(block, sides, width, periodic):
    for axis, dim in sides:
        count = lax.axis_size(axis)
        forward = [(i, i + 1) for i in range(count - 1)]
        if periodic:
            forward.append((count - 1, 0))
        backward = [(target, source) for source, target in forward]
        low = lax.ppermute(
            lax.slice_in_dim(block, block.shape[dim] - width, None, axis=dim), axis, forward
        )
        high = lax.ppermute(lax.slice_in_dim(block, 0, width, axis=dim), axis, backward)
        block = jnp.concatenate([low, block, high], axis=dim)
    return block


def basis_table(modes, cells, azimuth_total):
    frequency = (modes + 1) // 2
    phase = frequency[:, None] * (2 * cells[None, :] + 1) % (2 * azimuth_total)
    angle = phase.astype(jnp.float32) * (math.pi / azimuth_total)
    return jnp.where((modes % 2 == 1)[:, None], jnp.sin(angle), jnp.cos(angle))


def mode_weight(modes, azimuth_total):
    single = (modes == 0) | (modes == azimuth_total - 1)
    return jnp.where(single, 1.0, 2.0).astype(jnp.float32) / azimuth_total


def radius_column(radial_cells):
    index = jnp.arange(radial_cells).astype(jnp.float32)
    return (1.0 - (radial_cells - index - 0.5) * RADIAL_STEP)[:, None]


def advance(
    center_b,
    center_u,
    radial_b,
    radial_u,
    azimuth_b,
    azimuth_u,
    axial_b,
    axial_u,
    radius,
    angle_step,
):
    inv_radial = 1.0 / (2.0 * RADIAL_STEP)
    inv_azimuth = 1.0 / (2.0 * radius * angle_step)
    inv_axial = 1.0 / (2.0 * AXIAL_STEP)
    grad_b = (
        (radial_b[0] - radial_b[1]) * inv_radial,
        (azimuth_b[0] - azimuth_b[1]) * inv_azimuth,
        (axial_b[0] - axial_b[1]) * inv_axial,
    )
    grad_u = (
        (radial_u[0] - radial_u[1]) * inv_radial,
        (azimuth_u[0] - azimuth_u[1]) * inv_azimuth,
        (axial_u[0] - axial_u[1]) * inv_axial,
    )
    laplace = (radial_b[0] - 2.0 * center_b + radial_b[1]) / RADIAL_STEP**2
    laplace = laplace + grad_b[0] / radius
    laplace = laplace + (azimuth_b[0] - 2.0 * center_b + azimuth_b[1]) / (radius * angle_step) ** 2
    laplace = laplace + (axial_b[0] - 2.0 * center_b + axial_b[1]) / AXIAL_STEP**2
    carried = center_u[0] * grad_b[0] + center_u[1] * grad_b[1] + center_u[2] * grad_b[2]
    stretched = center_b[0] * grad_u[0] + center_b[1] * grad_u[1] + center_b[2] * grad_u[2]
    return center_b + TIME_STEP * (DIFFUSIVITY * laplace - carried + stretched)


def shards(magnetic, velocity, wall_response, mode_slots, wall_layers):
    axial_cells = magnetic.shape[1]
    radial_cells = magnetic.shape[2]
    azimuth_cells = magnetic.shape[3]
    azimuth_total = mode_slots.shape[0]
    mode_count = wall_response.shape[0]
    region_index = lax.axis_index("region")
    slab_index = lax.axis_index("slab")
    trace = magnetic[1:3, :, radial_cells - 1, :]
    trace_flat = trace.reshape(2 * axial_cells, azimuth_cells)
    local_cells = region_index * azimuth_cells + jnp.arange(azimuth_cells, dtype=jnp.int32)
    own_modes = lax.dynamic_slice_in_dim(mode_slots, region_index * azimuth_cells, azimuth_cells)
    table = basis_table(mode_slots, local_cells, azimuth_total)
    coefficients = lax.psum_scatter(
        jnp.dot(table, trace_flat.T, precision=HIGHEST), "region", scatter_dimension=0, tiled=True
    )
    by_mode = coefficients.reshape(azimuth_cells, 2, axial_cells)
    all_axial = lax.all_gather(by_mode, "slab", axis=2, tiled=True)
    mine = lax.dynamic_slice_in_dim(all_axial, slab_index * mode_count, mode_count, 0)
    applied = jnp.einsum("szy,scy->scz", wall_response, mine, precision=HIGHEST)
    all_slots = lax.all_gather(applied, "slab", axis=0, tiled=True)
    returned = lax.dynamic_slice_in_dim(all_slots, slab_index * axial_cells, axial_cells, 2)
    returned_flat = returned.reshape(azimuth_cells, 2 * axial_cells)
    scaled = returned_flat * mode_weight(own_modes, azimuth_total)[:, None]
    cells = jnp.arange(azimuth_cells * lax.axis_size("region"), dtype=jnp.int32)
    table = basis_table(own_modes, cells, azimuth_total)
    flux_rows = lax.psum_scatter(
        jnp.dot(table.T, scaled, precision=HIGHEST), "region", scatter_dimension=0, tiled=True
    )
    wall_flux = flux_rows.reshape(azimuth_cells, 2, axial_cells).transpose(1, 2, 0)
    thickness = wall_layers.astype(jnp.float32) / LW
    ghost = jnp.concatenate(
        [magnetic[0:1, :, radial_cells - 1, :], trace - thickness * wall_flux], 0
    )
    both = jnp.concatenate([magnetic, velocity], 0)
    axial_ext = with_halo(both, (("slab", 1),), 1, False)
    azimuth_ext = with_halo(both, (("region", 3),), 1, True)
    outer_edge = jnp.concatenate([ghost, velocity[:, :, radial_cells - 1, :]], 0)
    radial_ext = jnp.concatenate([both[:, :, :1], both, outer_edge[:, :, None]], 2)
    radial_b = (radial_ext[:3, :, 2:], radial_ext[:3, :, :-2])
    radial_u = (radial_ext[3:, :, 2:], radial_ext[3:, :, :-2])
    azimuth_b = (azimuth_ext[:3, ..., 2:], azimuth_ext[:3, ..., :-2])
    azimuth_u = (azimuth_ext[3:, ..., 2:], azimuth_ext[3:, ..., :-2])
    axial_b = (axial_ext[:3, 2:], axial_ext[:3, :-2])
    axial_u = (axial_ext[3:, 2:], axial_ext[3:, :-2])
    radius = radius_column(radial_cells)
    angle_step = 2.0 * math.pi / azimuth_total
    magnetic_next = advance(
        magnetic,
        velocity,
        radial_b,
        radial_u,
        azimuth_b,
        azimuth_u,
        axial_b,
        axial_u,
        radius,
        angle_step,
    )
    return (magnetic_next, wall_flux)


def solution(mesh):
    placed = (
        P(None, "slab", None, "region"),
        P(None, "slab", None, "region"),
        P(("region", "slab"), None, None),
        P(),
        P("region"),
    )
    return jax.shard_map(
        shards,
        mesh=mesh,
        in_specs=placed,
        out_specs=(P(None, "slab", None, "region"), P(None, "slab", "region")),
        check_vma=False,
    )
```

profile of v0, /device:TPU:0, one launch (start us, length us, event | category | flops | bytes accessed | tf_op | source)
XLA Modules:
  0.0 167.0 jit_solution(17377935890248300683)
XLA Ops:
  8.8 0.9 slice.91
  9.7 1.4 fusion.22
  11.2 3.4 %copy.99 = f32[3,16,64,128]{2,1,3,0:T(8,128)} copy(f32[3,16,64,128]{3,2,1,0:T(8,128)} %param.5) | data formatting | bytes 3145728 | tf_op args[0]
  14.6 3.3 %copy.80 = f32[3,16,64,128]{2,1,3,0:T(8,128)} copy(f32[3,16,64,128]{3,2,1,0:T(8,128)} %param.6) | data formatting | bytes 3145728 | tf_op args[1]
  17.9 3.6 %fusion.15 = (f32[6,1,64,128]{2,1,3,0:T(1,128)S(1)}, f32[6,1,64,128]{2,1,3,0:T(1,128)S(1)}) fusion(f32[3,16,64,128]{2,1,3,0:T(8,128)} %copy.99, f32[3,16,64,128]{2,1,3,0:T(8,128)} %copy.80), kind=kLoop, calls=%fused_computation.45 | loop fusion | flops 98304 | bytes 3538944 | tf_op jit(solution)/shard_map/concatenate | solution.py:118
  21.5 0.9 copy.89
  22.4 1.3 collective-permute-start.2
  23.7 0.9 copy.91
  24.6 3.8 %collective-permute-start.3 = (f32[6,1,64,128]{3,2,1,0:T(8,128)}, f32[6,1,64,128]{3,2,1,0:T(8,128)}, u32[]{:S(2)}, u32[]{:S(2)}) collective-permute-start(f32[6,1,64,128]{3,2,1,0:T(8,128)} %copy.91), channel_id=1, source_target_pairs={{0,1},{1,2},{2,3},{3,4},{4,5},{5,6},{6,7},{7,8},{8,9},{9,10},{10,1... | collective-permute-start | bytes 589832 | tf_op jit(solution)/shard_map/ppermute | solution.py:25
  28.5 1.4 fusion.52
  29.9 3.0 %collective-permute-start = (f32[6,16,64,1]{2,1,3,0:T(8,128)}, f32[6,16,64,1]{2,1,3,0:T(8,128)}, u32[]{:S(2)}, u32[]{:S(2)}) collective-permute-start(f32[6,16,64,1]{2,1,3,0:T(8,128)} %get-tuple-element.12), channel_id=1, source_target_pairs={{16,0},{0,16},{17,1},{1,17},{18,2},{2,18},{19,3},{3,19},{20,4},{4,... | collective-permute-start | bytes 73736 | tf_op jit(solution)/shard_map/ppermute | solution.py:28
  33.1 1.0 slice.92
  34.9 6.4 %fusion = f32[6,16,1,128]{2,1,3,0:T(8,128)} fusion(f32[3,16,64,128]{2,1,3,0:T(8,128)} %copy.99, f32[3,16,64,128]{2,1,3,0:T(8,128)} %copy.80), kind=kLoop, calls=%fused_computation.8 | loop fusion | flops 12288 | bytes 3194880 | tf_op jit(solution)/shard_map/concatenate | solution.py:118
  41.3 1.3 multiply_bitcast_fusion.3
  43.2 1.2 multiply_bitcast_fusion.1
  44.4 1.5 copy.93
  46.0 2.4 %copy.94 = f32[16,64,128]{1,0,2:T(8,128)} copy(f32[16,64,128]{2,1,0:T(8,128)} %get-tuple-element.18) | data formatting | bytes 1048576 | tf_op jit(solution)/shard_map/mul | solution.py:79
  48.4 2.4 %copy.95 = f32[16,64,128]{1,0,2:T(8,128)} copy(f32[16,64,128]{2,1,0:T(8,128)} %get-tuple-element.17) | data formatting | bytes 1048576 | tf_op jit(solution)/shard_map/mul | solution.py:79
  50.8 2.4 %copy.96 = f32[16,64,128]{1,0,2:T(8,128)} copy(f32[16,64,128]{2,1,0:T(8,128)} %get-tuple-element.19) | data formatting | bytes 1048576 | tf_op jit(solution)/shard_map/mul | solution.py:80
  53.3 2.4 %copy.97 = f32[16,64,128]{1,0,2:T(8,128)} copy(f32[16,64,128]{2,1,0:T(8,128)} %get-tuple-element.20) | data formatting | bytes 1048576 | tf_op jit(solution)/shard_map/mul | solution.py:80
  55.7 2.4 %copy.98 = f32[16,64,128]{1,0,2:T(8,128)} copy(f32[16,64,128]{2,1,0:T(8,128)} %get-tuple-element.21) | data formatting | bytes 1048576 | tf_op jit(solution)/shard_map/mul | solution.py:80
  58.9 22.8 %all_gather.6 = f32[128,2,256]{0,1,2:T(2,128)S(1)} all-gather(f32[128,2,16]{0,1,2:T(2,128)S(1)} %copy.83), channel_id=1, replica_groups=mesh['region'=2,'slab'=16] {'slab'}, dimensions={2}, use_global_device_ids=true | all-gather | bytes 278528 | tf_op jit(solution)/shard_map/all_gather | solution.py:101
  82.1 1.8 %fusion.67 = f32[8,2,256]{2,1,0:T(2,128)S(1)} fusion(f32[8,2,256]{2,1,0:T(2,128)S(1)} %copy.103, f32[8,256,256]{2,1,0:T(8,128)S(1)} %copy-done), kind=kOutput, calls=%fused_computation.132 | convolution fusion | flops 12582912 | bytes 2129920 | tf_op jit(solution)/shard_map/szy,scy->scz/dot_general | solution.py:103
  84.0 18.3 %all_gather.7 = f32[128,2,256]{2,1,0:T(2,128)S(1)} all-gather(f32[8,2,256]{2,1,0:T(2,128)S(1)} %fusion.67), channel_id=1, replica_groups=mesh['region'=2,'slab'=16] {'slab'}, dimensions={0}, use_global_device_ids=true | all-gather | bytes 278528 | tf_op jit(solution)/shard_map/all_gather | solution.py:104
  102.6 1.4 fusion.27
  104.0 8.4 %reduce-scatter.5.cloned.1.call-done = f32[128,32]{0,1:T(8,128)} async-done(((f32[256,32]{0,1:T(8,128)}), f32[128,32]{0,1:T(8,128)}) %reduce-scatter.5.cloned.1.call-update) | async-done | bytes 16400 | tf_op jit(solution)/shard_map/reduce_scatter | solution.py:110
  113.2 4.2 %copy.87 = f32[6,16,1,128]{2,1,3,0:T(8,128)} copy(f32[6,16,1,128]{3,1,0,2:T(8,128)S(1)} %maximum_bitcast_fusion) | data formatting | bytes 98304 | tf_op jit(solution)/shard_map/broadcast_in_dim | solution.py:122
  117.4 14.5 %pad_maximum_fusion = (f32[6,16,65,128]{2,1,3,0:T(8,128)}, f32[6,16,65,128]{2,1,3,0:T(8,128)}) fusion(f32[6,16,1,128]{2,1,3,0:T(8,128)} %copy.87, f32[3,16,64,128]{2,1,3,0:T(8,128)} %copy.80, f32[3,16,64,128]{2,1,3,0:T(8,128)} %copy.99, f32[6,16,1,128]{2,1,3,0:T(8,128)} %fusion), kind=kLoop, calls=%fused_computation.9 | loop fusion | flops 3194880 | bytes 9633792 | tf_op jit(solution)/shard_map/concatenate | solution.py:122
  131.9 1.2 copy.90
  133.1 1.8 %copy.92 = f32[6,1,64,128]{2,1,3,0:T(1,128)} copy(f32[6,1,64,128]{3,2,1,0:T(8,128)} %collective-permute-done.3) | data formatting | bytes 393216 | tf_op jit(solution)/shard_map/ppermute | solution.py:25
  134.9 22.0 %fusion.6 = f32[3,16,64,128]{2,1,3,0:T(8,128)} fusion(f32[3,16,64,128]{2,1,3,0:T(8,128)} %copy.99, f32[6,1,64,128]{2,1,3,0:T(1,128)} %copy.92, f32[3,16,64,128]{2,1,3,0:T(8,128)} %copy.80, f32[6,1,64,128]{2,1,3,0:T(1,128)S(1)} %copy.90, f32[6,16,64,1]{2,1,3,0:T(8,128)} %collective-permute-done.1, f32[6,16,64,1]{2,1,3,0:T(8,128)} %collective-permute-done, ...), kind=kLoop, calls=%fused_computation.17 | loop fusion | flops 21233664 | bytes 14598912 | tf_op jit(solution)/shard_map/add | solution.py:81
  156.9 3.2 %copy.100 = f32[3,16,64,128]{3,2,1,0:T(8,128)} copy(f32[3,16,64,128]{2,1,3,0:T(8,128)} %fusion.6) | data formatting | bytes 3145728
  (39 shorter events, 5.7 us)
Async XLA Ops:
  7.2 75.0 %copy-start = (f32[8,256,256]{2,1,0:T(8,128)S(1)}, f32[8,256,256]{2,1,0:T(8,128)}, u32[]{:S(2)}) copy-start(f32[8,256,256]{2,1,0:T(8,128)} %param.7) | copy-start | bytes 6291460
  7.2 51.0 %reduce-scatter.3.cloned.1.call-start = ((), (), s32[]{:S(2)}) async-start(), calls=%async_computation.2 | async-start | bytes 49152 | tf_op jit(solution)/shard_map/reduce_scatter | solution.py:97
  11.1 101.3 %reduce-scatter.5.cloned.1.call-start = ((), (), s32[]{:S(2)}) async-start(), calls=%async_computation.3 | async-start | bytes 49152 | tf_op jit(solution)/shard_map/reduce_scatter | solution.py:110
  22.4 109.4 %collective-permute-start.2 = (f32[6,1,64,128]{3,2,1,0:T(8,128)}, f32[6,1,64,128]{3,2,1,0:T(8,128)}, u32[]{:S(2)}, u32[]{:S(2)}) collective-permute-start(f32[6,1,64,128]{3,2,1,0:T(8,128)} %copy.89), channel_id=1, source_target_pairs={{1,0},{2,1},{3,2},{4,3},{5,4},{6,5},{7,6},{8,7},{9,8},{10,9},{11,1... | collective-permute-start | bytes 589832 | tf_op jit(solution)/shard_map/ppermute | solution.py:28
  24.6 8.3 %copy-start.3 = (s32[256]{0:T(256)S(1)}, s32[256]{0:T(256)}, u32[]{:S(2)}) copy-start(s32[256]{0:T(256)} %param.8) | copy-start | bytes 3076
  24.6 108.4 %collective-permute-start.3 = (f32[6,1,64,128]{3,2,1,0:T(8,128)}, f32[6,1,64,128]{3,2,1,0:T(8,128)}, u32[]{:S(2)}, u32[]{:S(2)}) collective-permute-start(f32[6,1,64,128]{3,2,1,0:T(8,128)} %copy.91), channel_id=1, source_target_pairs={{0,1},{1,2},{2,3},{3,4},{4,5},{5,6},{6,7},{7,8},{8,9},{9,10},{10,1... | collective-permute-start | bytes 589832 | tf_op jit(solution)/shard_map/ppermute | solution.py:25
  29.9 105.0 %collective-permute-start = (f32[6,16,64,1]{2,1,3,0:T(8,128)}, f32[6,16,64,1]{2,1,3,0:T(8,128)}, u32[]{:S(2)}, u32[]{:S(2)}) collective-permute-start(f32[6,16,64,1]{2,1,3,0:T(8,128)} %get-tuple-element.12), channel_id=1, source_target_pairs={{16,0},{0,16},{17,1},{1,17},{18,2},{2,18},{19,3},{3,19},{20,4},{4,... | collective-permute-start | bytes 73736 | tf_op jit(solution)/shard_map/ppermute | solution.py:28
  32.9 102.0 %collective-permute-start.1 = (f32[6,16,64,1]{2,1,3,0:T(8,128)}, f32[6,16,64,1]{2,1,3,0:T(8,128)}, u32[]{:S(2)}, u32[]{:S(2)}) collective-permute-start(f32[6,16,64,1]{2,1,3,0:T(8,128)} %get-tuple-element.13), channel_id=1, source_target_pairs={{0,16},{16,0},{1,17},{17,1},{2,18},{18,2},{3,19},{19,3},{4,20},{20... | collective-permute-start | bytes 73736 | tf_op jit(solution)/shard_map/ppermute | solution.py:25
  34.9 6.4 %copy-start.1 = (f32[3,16,64,128]{3,2,1,0:T(8,128)S(1)}, f32[3,16,64,128]{3,2,1,0:T(8,128)}, u32[]{:S(2)}) copy-start(f32[3,16,64,128]{3,2,1,0:T(8,128)} %param.6) | copy-start | bytes 4718596
  41.3 2.0 %copy-start.2 = (f32[3,16,64,128]{3,2,1,0:T(8,128)S(1)}, f32[3,16,64,128]{3,2,1,0:T(8,128)}, u32[]{:S(2)}) copy-start(f32[3,16,64,128]{3,2,1,0:T(8,128)} %param.5) | copy-start | bytes 4718596
  41.3 3.2 %copy-start.4 = (s32[128]{0:T(128)S(1)}, s32[128]{0:T(128)}, u32[]{:S(2)}) copy-start(s32[128]{0:T(128)} %param.9) | copy-start | bytes 1540
Sparse Core Ops, SparseCore 0:
  11.3 12.5 reduce-scatter.2
  104.1 8.2 reduce-scatter.4
where the time goes:
time: 168 us; the launch traced here: 167 us
  other arithmetic  52.9 us (31%)
  blocking collectives  41.1 us (24%)
  local copies, waits for them, and re-layouts  37.5 us (22%)
  between operations  14.1 us (8%)
  waiting for transfers between devices  8.46 us (5%)
  starting transfers between devices  8.2 us (5%)
  matrix products  4.66 us (3%)
    all_gather x1, blocking collectives, shards(): all_axial = lax.all_gather(by_mode, 'slab', axis=2, tiled=True)  22.8 us
    add x1, other arithmetic, advance(): return center_b + TIME_STEP * (DIFFUSIVITY * laplace - carried + stretched)  22 us
    all_gather x1, blocking collectives, shards(): all_slots = lax.all_gather(applied, 'slab', axis=0, tiled=True)  18.3 us
    concatenate x1, other arithmetic, shards(): jnp.concatenate([both[:, :, :1], both, outer_edge[:, :, None]], 2)  14.5 us
    concatenate x3, other arithmetic, shards(): both = jnp.concatenate([magnetic, velocity], 0)  11.4 us
    unnamed x15, local copies, waits for them, and re-layouts  10.8 us
    reduce_scatter x1, waiting for transfers between devices, shards(): lax.psum_scatter(jnp.dot(table.T, scaled, precision=HIGHEST), 'region', s...  8.42 us
    ppermute x2, starting transfers between devices, with_halo(): lax.ppermute(lax.slice_in_dim(block, 0, width, axis=dim), axis, backward)  4.24 us
  transfers between devices with their start and end apart: 6, of which 1 were waited for; matrix products, arithmetic and copies ran while one was open for 39% of the time, Pallas kernels for 0%

commit v1 on v0

v1 whole, which is shorter than its diff:
```python
import functools
import math

import jax
import jax.numpy as jnp
from jax import lax
from jax.experimental import pallas as pl
from jax.experimental.pallas import tpu as pltpu
from jax.sharding import PartitionSpec as P

LW = 8
TIME_STEP = 0.0003
DIFFUSIVITY = 0.001
RADIAL_STEP = 1.0 / 384.0
AXIAL_STEP = 1.0 / 768.0
HIGHEST = lax.Precision.HIGHEST
MESH = pl.DeviceIdType.MESH
F32 = jnp.float32
BF16 = jnp.bfloat16

PAD = 8
LANES = 128


def iota(shape, dim):
    return lax.broadcasted_iota(jnp.int32, shape, dim)


def split(x):
    hi = x.astype(BF16)
    return hi, (x - hi.astype(F32)).astype(BF16)


def sine(t):
    s = t * t
    value = 1.0 / math.factorial(13)
    for n in (11, 9, 7, 5, 3, 1):
        sign = 1.0 if (n // 2) % 2 == 0 else -1.0
        value = value * s + sign / math.factorial(n)
    return value * t


def exact_dot(a, b, contract):
    return lax.dot_general(
        a, b, ((contract[0], contract[1]), ((), ())), precision=HIGHEST, preferred_element_type=F32
    )


def step_kernel(
    regions,
    slabs,
    mode_ref,
    layer_ref,
    mag_hbm,
    vel_hbm,
    wall_hbm,
    next_hbm,
    flux_ref,
    b_s,
    u_s,
    out_s,
    wall_s,
    whi_s,
    wlo_s,
    table_s,
    weighted_s,
    trace_s,
    blocks_s,
    radial_s,
    row_s,
    spread_s,
    send1,
    recv1,
    send2,
    recv2,
    pack_s,
    around_s,
    halo_s,
    load_sem,
    store_sem,
    a2a_send,
    a2a_recv,
    ax_send,
    ax_recv,
    az_send,
    az_recv,
):
    count = regions * slabs
    radial = mag_hbm.shape[2]
    axial = mag_hbm.shape[1]
    azimuth_total = mode_ref.shape[1]
    mode_count, nz, _ = wall_hbm.shape
    rows_each = send1.shape[1]
    slot_rows = count * rows_each
    per_row = LANES // (2 * axial)
    region = lax.axis_index("region")
    slab = lax.axis_index("slab")
    me = region * slabs + slab
    cells = pl.ds(PAD, radial)

    load_b = pltpu.make_async_copy(mag_hbm, b_s.at[:, 1 : axial + 1, cells, :], load_sem.at[0])
    load_u = pltpu.make_async_copy(vel_hbm, u_s.at[:, 1 : axial + 1, cells, :], load_sem.at[1])
    load_w = pltpu.make_async_copy(wall_hbm, wall_s, load_sem.at[2])
    load_b.start()
    load_u.start()
    load_w.start()

    barrier = pltpu.get_barrier_semaphore()

    @pl.loop(1, count)
    def _(i):
        other = lax.rem(me + i, count)
        pl.semaphore_signal(
            barrier,
            inc=1,
            device_id=(other // slabs, lax.rem(other, slabs)),
            device_id_type=MESH,
        )

    modes = mode_ref[...].astype(F32)
    padded = table_s.shape[0]
    shape = (padded, azimuth_total)
    chosen = jnp.where(iota(shape, 1) // per_row == iota(shape, 0), modes, 0.0)
    shape = (azimuth_total, per_row * LANES)
    picks = jnp.where(lax.rem(iota(shape, 0), per_row) == iota(shape, 1) // LANES, 1.0, 0.0)
    mode = exact_dot(chosen, picks, ((1,), (0,)))
    half = jnp.floor(mode * 0.5)
    odd = mode - 2.0 * half
    cell = region * LANES + lax.rem(iota(mode.shape, 1), LANES)
    turn = (half + odd) * (2 * cell + 1).astype(F32) - odd * (azimuth_total // 2)
    turn = turn * (0.5 / azimuth_total)
    turn = turn - jnp.floor(turn + 0.5)
    table = sine((0.25 - jnp.abs(turn)) * (2.0 * math.pi))
    table_s[...] = table
    single = (mode == 0.0) | (mode == azimuth_total - 1.0)
    weighted_s[...] = table * (jnp.where(single, 1.0, 2.0) / azimuth_total)

    shape = (radial, LANES)
    radius = 1.0 - (radial - iota(shape, 0).astype(F32) - 0.5) * RADIAL_STEP
    inverse = 1.0 / radius
    angle_step = 2.0 * math.pi / azimuth_total
    kr = TIME_STEP * DIFFUSIVITY / RADIAL_STEP**2
    kz = TIME_STEP * DIFFUSIVITY / AXIAL_STEP**2
    ar = TIME_STEP / (2.0 * RADIAL_STEP)
    az = TIME_STEP / (2.0 * AXIAL_STEP)
    kp = inverse * inverse * (TIME_STEP * DIFFUSIVITY / angle_step**2)
    radial_s[0] = inverse * (TIME_STEP / (2.0 * angle_step))
    radial_s[1] = kp
    radial_s[2] = inverse * (TIME_STEP * DIFFUSIVITY / (2.0 * RADIAL_STEP))
    radial_s[3] = (1.0 - 2.0 * kr - 2.0 * kz) - 2.0 * kp

    if slot_rows < padded:
        row_s[...] = jnp.zeros(row_s.shape, F32)
    blocks_s[...] = jnp.zeros(blocks_s.shape, F32)

    load_b.wait()
    for c in range(2):
        for z in range(axial):
            at = c * axial + z
            trace_s[at : at + 1, :] = b_s[c + 1, z + 1, PAD + radial - 1 : PAD + radial, :]
    trace = trace_s[...]
    for q in range(per_row):
        blocks_s[2 * axial * q : 2 * axial * (q + 1), LANES * q : LANES * (q + 1)] = trace
    coefficients = exact_dot(table_s[0:slot_rows, :], blocks_s[...], ((1,), (1,)))
    for o in range(count):
        send1[o] = coefficients[rows_each * o : rows_each * (o + 1)]
    recv1[pl.ds(me, 1)] = send1[pl.ds(me, 1)]

    pl.semaphore_wait(barrier, count - 1)

    @pl.loop(1, count)
    def _(i):
        other = lax.rem(me + i, count)
        pltpu.make_async_remote_copy(
            src_ref=send1.at[other],
            dst_ref=recv1.at[me],
            send_sem=a2a_send.at[0],
            recv_sem=a2a_recv.at[0],
            device_id=(other // slabs, lax.rem(other, slabs)),
            device_id_type=MESH,
        ).start()

    load_u.wait()

    def axial_copy(field, at, up):
        return pltpu.make_async_remote_copy(
            src_ref=field.at[:, pl.ds(axial if up else 1, 1), cells, :],
            dst_ref=field.at[:, pl.ds(0 if up else axial + 1, 1), cells, :],
            send_sem=ax_send.at[at],
            recv_sem=ax_recv.at[at],
            device_id=(region, slab + 1 if up else slab - 1),
            device_id_type=MESH,
        )

    up_copies = [axial_copy(b_s, 0, True), axial_copy(u_s, 1, True)]
    down_copies = [axial_copy(b_s, 2, False), axial_copy(u_s, 3, False)]

    lane = iota((radial, LANES), 1)
    pair = lax.rem(lane + 1, LANES) // 2

    for f, field in enumerate((b_s, u_s)):
        def pack(z, total, field=field):
            for c in range(3):
                at = c * axial + z
                plane = field[c, z + 1, PAD : PAD + radial, :]
                total = jnp.where(pair == at, pltpu.roll(plane, 2 * at, 1), total)
                field[c, z + 1, PAD - 1 : PAD, :] = plane[0:1]
                field[c, z + 1, PAD + radial : PAD + radial + 1, :] = plane[radial - 1 : radial]
            return total

        pack_s[f] = lax.fori_loop(0, axial, pack, jnp.zeros((radial, LANES), F32))

    left = lax.rem(region + regions - 1, regions)
    right = lax.rem(region + 1, regions)

    def azimuth_copy(at, target):
        return pltpu.make_async_remote_copy(
            src_ref=pack_s,
            dst_ref=around_s.at[at],
            send_sem=az_send.at[at],
            recv_sem=az_recv.at[at],
            device_id=(target, slab),
            device_id_type=MESH,
        )

    azimuth_copies = [azimuth_copy(0, right)]
    if regions > 2:
        azimuth_copies.append(azimuth_copy(1, left))
    for copy in azimuth_copies:
        copy.start()

    @pl.when(slab < slabs - 1)
    def _():
        for copy in up_copies:
            copy.start()

    @pl.when(slab > 0)
    def _():
        for copy in down_copies:
            copy.start()

    @pl.when(slab == 0)
    def _():
        for field in (b_s, u_s):
            field[:, 0, PAD : PAD + radial, :] = jnp.zeros((3, radial, LANES), F32)

    @pl.when(slab == slabs - 1)
    def _():
        for field in (b_s, u_s):
            field[:, axial + 1, PAD : PAD + radial, :] = jnp.zeros((3, radial, LANES), F32)

    load_w.wait()
    for s in range(mode_count):
        whi_s[s], wlo_s[s] = split(wall_s[s])

    def wait_all(buffer, sem):
        part = buffer.at[pl.ds(0, count - 1)]
        pltpu.make_async_copy(part, part, sem).wait()

    wait_all(recv1, a2a_recv.at[0])
    shape = (axial, LANES)
    own_cell = lax.rem(iota(shape, 1), axial) == iota(shape, 0)
    for j in range(slabs):
        got = recv1[j]
        for g in range(1, regions):
            got = got + recv1[g * slabs + j]
        for r in range(rows_each):
            hi, lo = split(jnp.where(own_cell, got[r : r + 1], 0.0))
            spread_s[r, 0, axial * j : axial * (j + 1), :] = hi
            spread_s[r, 1, axial * j : axial * (j + 1), :] = lo
    shape = (LANES, LANES)
    group = jnp.where(iota(shape, 0) // axial == iota(shape, 1) // axial, 1.0, 0.0).astype(BF16)
    shape = (nz, LANES)
    own_lane = lax.rem(iota(shape, 1), axial) == lax.rem(iota(shape, 0), axial)
    lane_group = iota(shape, 1) // (2 * axial)
    for r in range(rows_each):
        hi = jnp.dot(spread_s[r, 0], group, preferred_element_type=F32).astype(BF16)
        lo = jnp.dot(spread_s[r, 1], group, preferred_element_type=F32).astype(BF16)
        both = jnp.concatenate([hi, lo], axis=1)
        total = jnp.zeros((nz, LANES), F32)
        for q in range(per_row):
            s = r * per_row + q
            first = jnp.dot(whi_s[s], both, preferred_element_type=F32)
            second = jnp.dot(wlo_s[s], hi, preferred_element_type=F32)
            answer = first[:, :LANES] + (first[:, LANES:] + second)
            total = jnp.where(own_lane & (lane_group == q), answer, total)
        message = jnp.sum(total.reshape(slabs, axial, LANES), axis=1)
        for j in range(slabs):
            send2[j, r : r + 1, :] = message[j : j + 1]
    recv2[pl.ds(me, 1)] = send2[pl.ds(slab, 1)]

    @pl.loop(1, count)
    def _(i):
        other = lax.rem(me + i, count)
        target = lax.rem(other, slabs)
        pltpu.make_async_remote_copy(
            src_ref=send2.at[target],
            dst_ref=recv2.at[me],
            send_sem=a2a_send.at[1],
            recv_sem=a2a_recv.at[1],
            device_id=(other // slabs, target),
            device_id_type=MESH,
        ).start()

    for copy in azimuth_copies:
        copy.wait()

    even = lax.rem(lane, 2) == 0
    for f in range(2):
        from_left = around_s[0, f]
        from_right = around_s[len(azimuth_copies) - 1, f]
        halo_s[f] = jnp.where(
            even, pltpu.roll(from_left, 1, 1), pltpu.roll(from_right, LANES - 1, 1)
        )

    @pl.when(slab < slabs - 1)
    def _():
        for copy in up_copies:
            copy.wait_send()
        for copy in down_copies:
            copy.wait_recv()

    @pl.when(slab > 0)
    def _():
        for copy in down_copies:
            copy.wait_send()
        for copy in up_copies:
            copy.wait_recv()

    depth = 16
    first_lane = iota((depth, LANES), 1) == 0
    last_lane = iota((depth, LANES), 1) == LANES - 1

    def advance(z, carry):
        for start in range(0, radial, depth):
            rows = slice(PAD + start, PAD + start + depth)
            above = slice(PAD + start + 1, PAD + start + depth + 1)
            below = slice(PAD + start - 1, PAD + start + depth - 1)
            here = slice(start, start + depth)
            ap = radial_s[0, here, :]
            kp = radial_s[1, here, :]
            k1 = radial_s[2, here, :]
            kc = radial_s[3, here, :]

            def around(f, c, center):
                shift = lax.rem(LANES - lax.rem(2 * (c * axial + z), LANES), LANES)
                halo = pltpu.roll(halo_s[f, here, :], shift, 1)
                before = jnp.where(first_lane, halo, pltpu.roll(center, 1, 1))
                after = jnp.where(last_lane, halo, pltpu.roll(center, LANES - 1, 1))
                return before, after

            b = [b_s[c, z + 1, rows, :] for c in range(3)]
            u = [u_s[c, z + 1, rows, :] for c in range(3)]
            ur, up, uz = ar * u[0] - k1, ap * u[1], az * u[2]
            br, bp, bz = ar * b[0], ap * b[1], az * b[2]
            r_next, r_last = kr - ur, kr + ur
            p_next, p_last = kp - up, kp + up
            z_next, z_last = kz - uz, kz + uz
            for c in range(3):
                before, after = around(0, c, b[c])
                value = b[c] * kc
                value += r_next * b_s[c, z + 1, above, :] + r_last * b_s[c, z + 1, below, :]
                value += p_next * after + p_last * before
                value += z_next * b_s[c, z + 2, rows, :] + z_last * b_s[c, z, rows, :]
                before, after = around(1, c, u[c])
                value += br * (u_s[c, z + 1, above, :] - u_s[c, z + 1, below, :])
                value += bp * (after - before)
                value += bz * (u_s[c, z + 2, rows, :] - u_s[c, z, rows, :])
                out_s[c, z, here, :] = value
        return carry

    lax.fori_loop(0, axial, advance, 0)
    top = radial - 8
    store_inner = pltpu.make_async_copy(
        out_s.at[:, :, 0:top, :], next_hbm.at[:, :, 0:top, :], store_sem.at[0]
    )
    store_inner.start()

    for z in range(axial):
        trace_s[z : z + 1, :] = u_s[0, z + 1, PAD + radial - 1 : PAD + radial, :]
    outer = kr + radial_s[2, radial - 1 : radial, :] - ar * trace_s[0:axial, :]
    thickness = layer_ref[...].astype(F32) * (1.0 / LW)
    wait_all(recv2, a2a_recv.at[1])
    for o in range(count):
        row_s[rows_each * o : rows_each * (o + 1), :] = recv2[o]
    turned = row_s[...].T
    flux = jnp.zeros((2 * axial, LANES), F32)
    for q in range(per_row):
        flux += exact_dot(
            turned[2 * axial * q : 2 * axial * (q + 1)],
            weighted_s[:, LANES * q : LANES * (q + 1)],
            ((1,), (0,)),
        )
    flux_ref[...] = flux
    change = flux * thickness * jnp.concatenate([outer, outer], axis=0)
    for c in range(2):
        for z in range(axial):
            at = c * axial + z
            out_s[c + 1, z, radial - 1 : radial, :] = (
                out_s[c + 1, z, radial - 1 : radial, :] - change[at : at + 1]
            )
    store_outer = pltpu.make_async_copy(
        out_s.at[:, :, top:radial, :], next_hbm.at[:, :, top:radial, :], store_sem.at[1]
    )
    store_outer.start()
    wait_all(recv1, a2a_send.at[0])
    wait_all(recv2, a2a_send.at[1])
    store_inner.wait()
    store_outer.wait()


def solution(mesh):
    regions = mesh.shape["region"]
    slabs = mesh.shape["slab"]
    count = regions * slabs

    def shards(magnetic, velocity, wall_response, mode_slots, wall_layers):
        _, axial, radial, azimuth = magnetic.shape
        azimuth_total = mode_slots.shape[0]
        mode_count, nz, _ = wall_response.shape
        rows_each = mode_count * 2 * axial // LANES
        per_row = LANES // (2 * axial)
        padded = max(LANES, count * rows_each)
        vmem = pl.BlockSpec(memory_space=pltpu.VMEM)
        hbm = pl.BlockSpec(memory_space=pl.ANY)
        field = pltpu.VMEM((3, axial + 2, radial + 2 * PAD, azimuth), F32)
        magnetic_next, flux = pl.pallas_call(
            functools.partial(step_kernel, regions, slabs),
            out_shape=(
                jax.ShapeDtypeStruct(magnetic.shape, F32),
                jax.ShapeDtypeStruct((2 * axial, azimuth), F32),
            ),
            in_specs=[vmem, vmem, hbm, hbm, hbm],
            out_specs=(hbm, vmem),
            scratch_shapes=[
                field,
                field,
                pltpu.VMEM(magnetic.shape, F32),
                pltpu.VMEM(wall_response.shape, F32),
                pltpu.VMEM(wall_response.shape, BF16),
                pltpu.VMEM(wall_response.shape, BF16),
                pltpu.VMEM((padded, per_row * LANES), F32),
                pltpu.VMEM((padded, per_row * LANES), F32),
                pltpu.VMEM((2 * axial, LANES), F32),
                pltpu.VMEM((LANES, per_row * LANES), F32),
                pltpu.VMEM((4, radial, LANES), F32),
                pltpu.VMEM((padded, LANES), F32),
                pltpu.VMEM((rows_each, 2, nz, LANES), BF16),
                pltpu.VMEM((count, rows_each, LANES), F32),
                pltpu.VMEM((count, rows_each, LANES), F32),
                pltpu.VMEM((slabs, rows_each, LANES), F32),
                pltpu.VMEM((count, rows_each, LANES), F32),
                pltpu.VMEM((2, radial, LANES), F32),
                pltpu.VMEM((2, 2, radial, LANES), F32),
                pltpu.VMEM((2, radial, LANES), F32),
                pltpu.SemaphoreType.DMA((3,)),
                pltpu.SemaphoreType.DMA((2,)),
                pltpu.SemaphoreType.DMA((2,)),
                pltpu.SemaphoreType.DMA((2,)),
                pltpu.SemaphoreType.DMA((4,)),
                pltpu.SemaphoreType.DMA((4,)),
                pltpu.SemaphoreType.DMA((2,)),
                pltpu.SemaphoreType.DMA((2,)),
            ],
            compiler_params=pltpu.CompilerParams(
                collective_id=0, has_side_effects=True, vmem_limit_bytes=48 * 1024 * 1024
            ),
            name="wall_step",
        )(
            mode_slots.reshape(1, azimuth_total),
            wall_layers.reshape(1, azimuth),
            magnetic,
            velocity,
            wall_response,
        )
        return magnetic_next, flux.reshape(2, axial, azimuth)

    placed = (
        P(None, "slab", None, "region"),
        P(None, "slab", None, "region"),
        P(("region", "slab"), None, None),
        P(),
        P("region"),
    )
    return jax.shard_map(
        shards,
        mesh=mesh,
        in_specs=placed,
        out_specs=(P(None, "slab", None, "region"), P(None, "slab", "region")),
        check_vma=False,
    )
```

time: 168 us -> 26.6 us (0.16)
  the two profiles are of different devices: /device:TPU:0 before, /device:TPU:1 now
where the time goes in v1:
time: 26.6 us; the launch traced here: 26.4 us
  Pallas kernels  19.8 us (74%)
  local copies, waits for them, and re-layouts  5.89 us (22%)
  between operations  0.65 us (2%)
    pallas_call x1, Pallas kernels, shards(): pl.pallas_call(functools.partial(step_kernel, regions, slabs), out_shape=...  19.8 us
    unnamed x10, local copies, waits for them, and re-layouts  5.89 us

profile of v1, /device:TPU:1, one launch (start us, length us, event | category | flops | bytes accessed | tf_op | source)
XLA Modules:
  0.0 26.4 jit_solution(10569778374655411680)
XLA Ops:
  0.6 0.0 copy-start
  0.6 1.4 %copy-done = f32[3,16,64,128]{3,2,1,0:T(8,128)S(1)} copy-done((f32[3,16,64,128]{3,2,1,0:T(8,128)S(1)}, f32[3,16,64,128]{3,2,1,0:T(8,128)}, u32[]{:S(2)}) %copy-start) | copy-done | bytes 1572888
  2.0 0.0 copy-start.1
  2.0 1.4 %copy-done.1 = f32[3,16,64,128]{3,2,1,0:T(8,128)S(1)} copy-done((f32[3,16,64,128]{3,2,1,0:T(8,128)S(1)}, f32[3,16,64,128]{3,2,1,0:T(8,128)}, u32[]{:S(2)}) %copy-start.1) | copy-done | bytes 1572888
  3.4 0.0 copy-start.2
  3.5 0.7 %copy-done.2 = s32[256]{0:T(256)S(1)} copy-done((s32[256]{0:T(256)S(1)}, s32[256]{0:T(256)}, u32[]{:S(2)}) %copy-start.2) | copy-done | bytes 1048
  4.1 0.0 copy-start.3
  4.1 0.7 %copy-done.3 = s32[128]{0:T(128)S(1)} copy-done((s32[128]{0:T(128)S(1)}, s32[128]{0:T(128)}, u32[]{:S(2)}) %copy-start.3) | copy-done | bytes 536
  4.8 19.8 %wall_step.1 = (f32[3,16,64,128]{3,2,1,0:T(8,128)S(1)}, f32[32,128]{1,0:T(8,128)S(1)}) custom-call(s32[1,256]{1,0:T(1,128)S(1)} %bitcast.4, s32[1,128]{1,0:T(1,128)S(1)} %bitcast.5, f32[3,16,64,128]{3,2,1,0:T(8,128)S(1)} %copy-done, f32[3,16,64,128]{3,2,1,0:T(8,128)S(1)} %copy-done.1, f32[8,256,256]{2,1,0:T(8,128)} %wall_hbm.1), custom_call_target="tpu_custom_call" | custom-call | tf_op jit(solution)/shard_map/wall_step/pallas_call | solution.py:427
  24.6 1.1 %copy.9 = f32[3,16,64,128]{3,2,1,0:T(8,128)} copy(f32[3,16,64,128]{3,2,1,0:T(8,128)S(1)} %get-tuple-element.8) | data formatting | bytes 3145728
  25.8 0.6 %copy.10 = f32[2,16,128]{2,1,0:T(8,128)} copy(f32[2,16,128]{2,1,0:T(8,128)S(1)} %bitcast.3) | data formatting | bytes 32768
Async XLA Ops:
  0.6 1.4 %copy-start = (f32[3,16,64,128]{3,2,1,0:T(8,128)S(1)}, f32[3,16,64,128]{3,2,1,0:T(8,128)}, u32[]{:S(2)}) copy-start(f32[3,16,64,128]{3,2,1,0:T(8,128)} %mag_hbm.1) | copy-start | bytes 4718596
  2.0 1.4 %copy-start.1 = (f32[3,16,64,128]{3,2,1,0:T(8,128)S(1)}, f32[3,16,64,128]{3,2,1,0:T(8,128)}, u32[]{:S(2)}) copy-start(f32[3,16,64,128]{3,2,1,0:T(8,128)} %vel_hbm.1) | copy-start | bytes 4718596
  3.4 0.7 %copy-start.2 = (s32[256]{0:T(256)S(1)}, s32[256]{0:T(256)}, u32[]{:S(2)}) copy-start(s32[256]{0:T(256)} %param.8) | copy-start | bytes 3076
  4.1 0.7 %copy-start.3 = (s32[128]{0:T(128)S(1)}, s32[128]{0:T(128)}, u32[]{:S(2)}) copy-start(s32[128]{0:T(128)} %param.9) | copy-start | bytes 1540

commit v2 on v1

--- a/solution.py
+++ b/solution.py
@@ -13,7 +13,6 @@
 DIFFUSIVITY = 0.001
 RADIAL_STEP = 1.0 / 384.0
 AXIAL_STEP = 1.0 / 768.0
-HIGHEST = lax.Precision.HIGHEST
 MESH = pl.DeviceIdType.MESH
 F32 = jnp.float32
 BF16 = jnp.bfloat16
@@ -38,12 +37,6 @@
         sign = 1.0 if (n // 2) % 2 == 0 else -1.0
         value = value * s + sign / math.factorial(n)
     return value * t
-
-
-def exact_dot(a, b, contract):
-    return lax.dot_general(
-        a, b, ((contract[0], contract[1]), ((), ())), precision=HIGHEST, preferred_element_type=F32
-    )
 
 
 def step_kernel(
@@ -54,20 +47,22 @@
     mag_hbm,
     vel_hbm,
     wall_hbm,
-    next_hbm,
-    flux_ref,
+    out_s,
+    row_s,
+    weight_hi,
+    weight_lo,
+    outer_s,
     b_s,
     u_s,
-    out_s,
+    mode_s,
+    layer_s,
     wall_s,
     whi_s,
     wlo_s,
-    table_s,
-    weighted_s,
     trace_s,
-    blocks_s,
+    block_hi,
+    block_lo,
     radial_s,
-    row_s,
     spread_s,
     send1,
     recv1,
@@ -77,7 +72,6 @@
     around_s,
     halo_s,
     load_sem,
-    store_sem,
     a2a_send,
     a2a_recv,
     ax_send,
@@ -88,7 +82,7 @@
     count = regions * slabs
     radial = mag_hbm.shape[2]
     axial = mag_hbm.shape[1]
-    azimuth_total = mode_ref.shape[1]
+    azimuth_total = mode_s.shape[1]
     mode_count, nz, _ = wall_hbm.shape
     rows_each = send1.shape[1]
     slot_rows = count * rows_each
@@ -101,8 +95,12 @@
     load_b = pltpu.make_async_copy(mag_hbm, b_s.at[:, 1 : axial + 1, cells, :], load_sem.at[0])
     load_u = pltpu.make_async_copy(vel_hbm, u_s.at[:, 1 : axial + 1, cells, :], load_sem.at[1])
     load_w = pltpu.make_async_copy(wall_hbm, wall_s, load_sem.at[2])
+    load_modes = pltpu.make_async_copy(mode_ref, mode_s, load_sem.at[3])
+    load_layers = pltpu.make_async_copy(layer_ref, layer_s, load_sem.at[4])
+    load_modes.start()
     load_b.start()
     load_u.start()
+    load_layers.start()
     load_w.start()
 
     barrier = pltpu.get_barrier_semaphore()
@@ -117,13 +115,22 @@
             device_id_type=MESH,
         )
 
-    modes = mode_ref[...].astype(F32)
-    padded = table_s.shape[0]
-    shape = (padded, azimuth_total)
-    chosen = jnp.where(iota(shape, 1) // per_row == iota(shape, 0), modes, 0.0)
+    block_hi[...] = jnp.zeros(block_hi.shape, BF16)
+    block_lo[...] = jnp.zeros(block_lo.shape, BF16)
     shape = (azimuth_total, per_row * LANES)
     picks = jnp.where(lax.rem(iota(shape, 0), per_row) == iota(shape, 1) // LANES, 1.0, 0.0)
-    mode = exact_dot(chosen, picks, ((1,), (0,)))
+    shape = (slot_rows, azimuth_total)
+    mine = iota(shape, 1) // per_row == iota(shape, 0)
+    load_modes.wait()
+    modes = mode_s[...].astype(F32)
+    tens = jnp.floor(modes * (1.0 / 32.0))
+    parts = [jnp.where(mine, part, 0.0) for part in (tens, modes - 32.0 * tens)]
+    parts = jnp.dot(
+        jnp.concatenate(parts, axis=0).astype(BF16),
+        picks.astype(BF16),
+        preferred_element_type=F32,
+    )
+    mode = 32.0 * parts[:slot_rows] + parts[slot_rows:]
     half = jnp.floor(mode * 0.5)
     odd = mode - 2.0 * half
     cell = region * LANES + lax.rem(iota(mode.shape, 1), LANES)
@@ -131,9 +138,42 @@
     turn = turn * (0.5 / azimuth_total)
     turn = turn - jnp.floor(turn + 0.5)
     table = sine((0.25 - jnp.abs(turn)) * (2.0 * math.pi))
-    table_s[...] = table
+    table_hi, table_lo = split(table)
+
+    load_b.wait()
+    for c in range(2):
+        for z in range(axial):
+            at = c * axial + z
+            trace_s[at : at + 1, :] = b_s[c + 1, z + 1, PAD + radial - 1 : PAD + radial, :]
+    trace_hi, trace_lo = split(trace_s[...])
+    for q in range(per_row):
+        block_hi[2 * axial * q : 2 * axial * (q + 1), LANES * q : LANES * (q + 1)] = trace_hi
+        block_lo[2 * axial * q : 2 * axial * (q + 1), LANES * q : LANES * (q + 1)] = trace_lo
+    both = jnp.concatenate([table_hi, table_lo], axis=0)
+    turned = (((1,), (1,)), ((), ()))
+    first = lax.dot_general(both, block_hi[...], turned, preferred_element_type=F32)
+    second = lax.dot_general(table_hi, block_lo[...], turned, preferred_element_type=F32)
+    coefficients = first[:slot_rows] + (first[slot_rows:] + second)
+    for o in range(count):
+        send1[o] = coefficients[rows_each * o : rows_each * (o + 1)]
+    recv1[pl.ds(me, 1)] = send1[pl.ds(me, 1)]
+
+    pl.semaphore_wait(barrier, count - 1)
+
+    @pl.loop(1, count)
+    def _(i):
+        other = lax.rem(me + i, count)
+        pltpu.make_async_remote_copy(
+            src_ref=send1.at[other],
+            dst_ref=recv1.at[me],
+            send_sem=a2a_send.at[0],
+            recv_sem=a2a_recv.at[0],
+            device_id=(other // slabs, lax.rem(other, slabs)),
+            device_id_type=MESH,
+        ).start()
+
     single = (mode == 0.0) | (mode == azimuth_total - 1.0)
-    weighted_s[...] = table * (jnp.where(single, 1.0, 2.0) / azimuth_total)
+    weight_hi[...], weight_lo[...] = split(table * (jnp.where(single, 1.0, 2.0) / azimuth_total))
 
     shape = (radial, LANES)
     radius = 1.0 - (radial - iota(shape, 0).astype(F32) - 0.5) * RADIAL_STEP
@@ -148,37 +188,6 @@
     radial_s[1] = kp
     radial_s[2] = inverse * (TIME_STEP * DIFFUSIVITY / (2.0 * RADIAL_STEP))
     radial_s[3] = (1.0 - 2.0 * kr - 2.0 * kz) - 2.0 * kp
-
-    if slot_rows < padded:
-        row_s[...] = jnp.zeros(row_s.shape, F32)
-    blocks_s[...] = jnp.zeros(blocks_s.shape, F32)
-
-    load_b.wait()
-    for c in range(2):
-        for z in range(axial):
-            at = c * axial + z
-            trace_s[at : at + 1, :] = b_s[c + 1, z + 1, PAD + radial - 1 : PAD + radial, :]
-    trace = trace_s[...]
-    for q in range(per_row):
-        blocks_s[2 * axial * q : 2 * axial * (q + 1), LANES * q : LANES * (q + 1)] = trace
-    coefficients = exact_dot(table_s[0:slot_rows, :], blocks_s[...], ((1,), (1,)))
-    for o in range(count):
-        send1[o] = coefficients[rows_each * o : rows_each * (o + 1)]
-    recv1[pl.ds(me, 1)] = send1[pl.ds(me, 1)]
-
-    pl.semaphore_wait(barrier, count - 1)
-
-    @pl.loop(1, count)
-    def _(i):
-        other = lax.rem(me + i, count)
-        pltpu.make_async_remote_copy(
-            src_ref=send1.at[other],
-            dst_ref=recv1.at[me],
-            send_sem=a2a_send.at[0],
-            recv_sem=a2a_recv.at[0],
-            device_id=(other // slabs, lax.rem(other, slabs)),
-            device_id_type=MESH,
-        ).start()
 
     load_u.wait()
 
@@ -370,43 +379,52 @@
         return carry
 
     lax.fori_loop(0, axial, advance, 0)
-    top = radial - 8
-    store_inner = pltpu.make_async_copy(
-        out_s.at[:, :, 0:top, :], next_hbm.at[:, :, 0:top, :], store_sem.at[0]
-    )
-    store_inner.start()
-
+    load_layers.wait()
     for z in range(axial):
         trace_s[z : z + 1, :] = u_s[0, z + 1, PAD + radial - 1 : PAD + radial, :]
     outer = kr + radial_s[2, radial - 1 : radial, :] - ar * trace_s[0:axial, :]
-    thickness = layer_ref[...].astype(F32) * (1.0 / LW)
+    outer_s[...] = outer * (layer_s[...].astype(F32) * (1.0 / LW))
     wait_all(recv2, a2a_recv.at[1])
     for o in range(count):
         row_s[rows_each * o : rows_each * (o + 1), :] = recv2[o]
-    turned = row_s[...].T
-    flux = jnp.zeros((2 * axial, LANES), F32)
-    for q in range(per_row):
-        flux += exact_dot(
-            turned[2 * axial * q : 2 * axial * (q + 1)],
-            weighted_s[:, LANES * q : LANES * (q + 1)],
-            ((1,), (0,)),
-        )
-    flux_ref[...] = flux
-    change = flux * thickness * jnp.concatenate([outer, outer], axis=0)
-    for c in range(2):
-        for z in range(axial):
-            at = c * axial + z
-            out_s[c + 1, z, radial - 1 : radial, :] = (
-                out_s[c + 1, z, radial - 1 : radial, :] - change[at : at + 1]
-            )
-    store_outer = pltpu.make_async_copy(
-        out_s.at[:, :, top:radial, :], next_hbm.at[:, :, top:radial, :], store_sem.at[1]
-    )
-    store_outer.start()
     wait_all(recv1, a2a_send.at[0])
     wait_all(recv2, a2a_send.at[1])
-    store_inner.wait()
-    store_outer.wait()
+
+
+def finish_kernel(
+    out_ref, row_ref, weight_hi, weight_lo, outer_ref, next_hbm, flux_hbm, edge_s, flux_s, sem
+):
+    _, axial, radial, _ = out_ref.shape
+    top = radial - 8
+    inner = pltpu.make_async_copy(
+        out_ref.at[:, :, 0:top, :], next_hbm.at[:, :, 0:top, :], sem.at[0]
+    )
+    inner.start()
+    hi, lo = split(row_ref[...].T)
+    flux = jnp.zeros((2 * axial, LANES), F32)
+    for q in range(LANES // (2 * axial)):
+        part = slice(2 * axial * q, 2 * axial * (q + 1))
+        lanes = slice(LANES * q, LANES * (q + 1))
+        flux += jnp.dot(hi[part], weight_hi[:, lanes], preferred_element_type=F32)
+        flux += jnp.dot(lo[part], weight_hi[:, lanes], preferred_element_type=F32)
+        flux += jnp.dot(hi[part], weight_lo[:, lanes], preferred_element_type=F32)
+    flux_s[...] = flux
+    store_flux = pltpu.make_async_copy(flux_s, flux_hbm, sem.at[1])
+    store_flux.start()
+    outer = outer_ref[...]
+    last = iota((8, LANES), 0) == 7
+    for z in range(axial):
+        edge_s[0, z] = out_ref[0, z, top:radial, :]
+    for c in range(2):
+        change = flux[axial * c : axial * (c + 1)] * outer
+        for z in range(axial):
+            edge = out_ref[c + 1, z, top:radial, :]
+            edge_s[c + 1, z] = jnp.where(last, edge - change[z : z + 1], edge)
+    store_edge = pltpu.make_async_copy(edge_s, next_hbm.at[:, :, top:radial, :], sem.at[2])
+    store_edge.start()
+    inner.wait()
+    store_flux.wait()
+    store_edge.wait()
 
 
 def solution(mesh):
@@ -420,31 +438,33 @@
         mode_count, nz, _ = wall_response.shape
         rows_each = mode_count * 2 * axial // LANES
         per_row = LANES // (2 * axial)
-        padded = max(LANES, count * rows_each)
+        slot_rows = count * rows_each
         vmem = pl.BlockSpec(memory_space=pltpu.VMEM)
-        hbm = pl.BlockSpec(memory_space=pl.ANY)
+        hbm = pl.BlockSpec(memory_space=pltpu.HBM)
         field = pltpu.VMEM((3, axial + 2, radial + 2 * PAD, azimuth), F32)
-        magnetic_next, flux = pl.pallas_call(
+        kept = pl.pallas_call(
             functools.partial(step_kernel, regions, slabs),
             out_shape=(
-                jax.ShapeDtypeStruct(magnetic.shape, F32),
-                jax.ShapeDtypeStruct((2 * axial, azimuth), F32),
+                pltpu.VMEM(magnetic.shape, F32),
+                pltpu.VMEM((slot_rows, LANES), F32),
+                pltpu.VMEM((slot_rows, per_row * LANES), BF16),
+                pltpu.VMEM((slot_rows, per_row * LANES), BF16),
+                pltpu.VMEM((axial, LANES), F32),
             ),
-            in_specs=[vmem, vmem, hbm, hbm, hbm],
-            out_specs=(hbm, vmem),
+            in_specs=[hbm] * 5,
+            out_specs=(vmem,) * 5,
             scratch_shapes=[
                 field,
                 field,
-                pltpu.VMEM(magnetic.shape, F32),
+                pltpu.VMEM((1, azimuth_total), jnp.int32),
+                pltpu.VMEM((1, azimuth), jnp.int32),
                 pltpu.VMEM(wall_response.shape, F32),
                 pltpu.VMEM(wall_response.shape, BF16),
                 pltpu.VMEM(wall_response.shape, BF16),
-                pltpu.VMEM((padded, per_row * LANES), F32),
-                pltpu.VMEM((padded, per_row * LANES), F32),
                 pltpu.VMEM((2 * axial, LANES), F32),
-                pltpu.VMEM((LANES, per_row * LANES), F32),
+                pltpu.VMEM((LANES, per_row * LANES), BF16),
+                pltpu.VMEM((LANES, per_row * LANES), BF16),
                 pltpu.VMEM((4, radial, LANES), F32),
-                pltpu.VMEM((padded, LANES), F32),
                 pltpu.VMEM((rows_each, 2, nz, LANES), BF16),
                 pltpu.VMEM((count, rows_each, LANES), F32),
                 pltpu.VMEM((count, rows_each, LANES), F32),
@@ -453,8 +473,7 @@
                 pltpu.VMEM((2, radial, LANES), F32),
                 pltpu.VMEM((2, 2, radial, LANES), F32),
                 pltpu.VMEM((2, radial, LANES), F32),
-                pltpu.SemaphoreType.DMA((3,)),
-                pltpu.SemaphoreType.DMA((2,)),
+                pltpu.SemaphoreType.DMA((5,)),
                 pltpu.SemaphoreType.DMA((2,)),
                 pltpu.SemaphoreType.DMA((2,)),
                 pltpu.SemaphoreType.DMA((4,)),
@@ -467,12 +486,33 @@
             ),
             name="wall_step",
         )(
-            mode_slots.reshape(1, azimuth_total),
-            wall_layers.reshape(1, azimuth),
-            magnetic,
-            velocity,
-            wall_response,
+            *(
+                pltpu.with_memory_space_constraint(x, pltpu.HBM)
+                for x in (
+                    mode_slots.reshape(1, azimuth_total),
+                    wall_layers.reshape(1, azimuth),
+                    magnetic,
+                    velocity,
+                    wall_response,
+                )
+            )
         )
+        magnetic_next, flux = pl.pallas_call(
+            finish_kernel,
+            out_shape=(
+                jax.ShapeDtypeStruct(magnetic.shape, F32),
+                jax.ShapeDtypeStruct((2 * axial, azimuth), F32),
+            ),
+            in_specs=[vmem] * 5,
+            out_specs=(hbm, hbm),
+            scratch_shapes=[
+                pltpu.VMEM((3, axial, 8, LANES), F32),
+                pltpu.VMEM((2 * axial, LANES), F32),
+                pltpu.SemaphoreType.DMA((3,)),
+            ],
+            compiler_params=pltpu.CompilerParams(vmem_limit_bytes=48 * 1024 * 1024),
+            name="wall_finish",
+        )(*(pltpu.with_memory_space_constraint(x, pltpu.VMEM) for x in kept))
         return magnetic_next, flux.reshape(2, axial, azimuth)
 
     placed = (

time: 26.6 us -> 20.9 us (0.79)
  local copies, waits for them, and re-layouts: 5.89 us -> 0 us
  Pallas kernels: 19.8 us -> 20.1 us
    unnamed x10 -> x0, local copies, waits for them, and re-layouts: 5.89 us -> none
    pallas_call x0 -> x1, Pallas kernels: none -> 1.17 us  [shards(): pl.pallas_call(finish_kernel, out_shape=(jax.ShapeDtypeStruct(magnetic.sh...]
    pallas_call x1, Pallas kernels: 19.8 us -> 19 us  [shards(): pl.pallas_call(functools.partial(step_kernel, regions, slabs), out_shape=...]
where the time goes in v2:
time: 20.9 us; the launch traced here: 20.8 us
  Pallas kernels  20.1 us (96%)
  between operations  0.64 us (3%)
    pallas_call x1, Pallas kernels, shards(): pl.pallas_call(functools.partial(step_kernel, regions, slabs), out_shape=...  19 us
    pallas_call x1, Pallas kernels, shards(): pl.pallas_call(finish_kernel, out_shape=(jax.ShapeDtypeStruct(magnetic.sh...  1.17 us

profile of v2, /device:TPU:1, one launch (start us, length us, event | category | flops | bytes accessed | tf_op | source)
XLA Modules:
  0.0 20.8 jit_solution(9608018550830789345)
XLA Ops:
  0.6 19.0 %wall_step.1 = (f32[3,16,64,128]{3,2,1,0:T(8,128)S(1)}, f32[64,128]{1,0:T(8,128)S(1)}, bf16[64,512]{1,0:T(8,128)(2,1)S(1)}, bf16[64,512]{1,0:T(8,128)(2,1)S(1)}, f32[16,128]{1,0:T(8,128)S(1)}) custom-call(s32[1,256]{1,0:T(1,128)} %bitcast.3, s32[1,128]{1,0:T(1,128)} %bitcast.4, f32[3,16,64,128]{3,2,1,0:T(8,128)} %mag_hbm.1, f32[3,16,64,128]{3,2,1,0:T(8,128)} %vel_hbm.1, ...), custom_call_target="tpu_custom_call" | custom-call | tf_op jit(solution)/shard_map/wall_step/pallas_call | solution.py:445
  19.6 1.2 %wall_finish.1 = (f32[3,16,64,128]{3,2,1,0:T(8,128)}, f32[32,128]{1,0:T(8,128)}) custom-call(f32[3,16,64,128]{3,2,1,0:T(8,128)S(1)} %get-tuple-element.9.out_ref, f32[64,128]{1,0:T(8,128)S(1)} %get-tuple-element.10.row_ref, bf16[64,512]{1,0:T(8,128)(2,1)S(1)} %get-tuple-element.11.weight_hi, bf16[64,512]{1,0:T(8,128)(2,1)S(1)} %get-tuple-element.12.weight_lo, ...), custom_call_target="tpu_custom_call" | custom-call | tf_op jit(solution)/shard_map/wall_finish/pallas_call | solution.py:500

commit v3 on v2

--- a/solution.py
+++ b/solution.py
@@ -59,6 +59,7 @@
     wall_s,
     whi_s,
     wlo_s,
+    edge_s,
     trace_s,
     block_hi,
     block_lo,
@@ -97,7 +98,11 @@
     load_w = pltpu.make_async_copy(wall_hbm, wall_s, load_sem.at[2])
     load_modes = pltpu.make_async_copy(mode_ref, mode_s, load_sem.at[3])
     load_layers = pltpu.make_async_copy(layer_ref, layer_s, load_sem.at[4])
+    load_trace = pltpu.make_async_copy(
+        mag_hbm.at[1:3, :, radial - 8 : radial, :], edge_s, load_sem.at[5]
+    )
     load_modes.start()
+    load_trace.start()
     load_b.start()
     load_u.start()
     load_layers.start()
@@ -105,15 +110,20 @@
 
     barrier = pltpu.get_barrier_semaphore()
 
-    @pl.loop(1, count)
-    def _(i):
-        other = lax.rem(me + i, count)
+    def each_other(act):
+        for step in range(regions):
+            its_region = lax.rem(region + step, regions)
+
+            @pl.loop(0 if step else 1, slabs)
+            def _(i, its_region=its_region):
+                act(its_region, lax.rem(slab + i, slabs))
+
+    def greet(its_region, its_slab):
         pl.semaphore_signal(
-            barrier,
-            inc=1,
-            device_id=(other // slabs, lax.rem(other, slabs)),
-            device_id_type=MESH,
+            barrier, inc=1, device_id=(its_region, its_slab), device_id_type=MESH
         )
+
+    each_other(greet)
 
     block_hi[...] = jnp.zeros(block_hi.shape, BF16)
     block_lo[...] = jnp.zeros(block_lo.shape, BF16)
@@ -140,11 +150,11 @@
     table = sine((0.25 - jnp.abs(turn)) * (2.0 * math.pi))
     table_hi, table_lo = split(table)
 
-    load_b.wait()
+    load_trace.wait()
     for c in range(2):
         for z in range(axial):
             at = c * axial + z
-            trace_s[at : at + 1, :] = b_s[c + 1, z + 1, PAD + radial - 1 : PAD + radial, :]
+            trace_s[at : at + 1, :] = edge_s[c, z, 7:8, :]
     trace_hi, trace_lo = split(trace_s[...])
     for q in range(per_row):
         block_hi[2 * axial * q : 2 * axial * (q + 1), LANES * q : LANES * (q + 1)] = trace_hi
@@ -160,17 +170,79 @@
 
     pl.semaphore_wait(barrier, count - 1)
 
-    @pl.loop(1, count)
-    def _(i):
-        other = lax.rem(me + i, count)
+    def send_coefficients(its_region, its_slab):
         pltpu.make_async_remote_copy(
-            src_ref=send1.at[other],
+            src_ref=send1.at[its_region * slabs + its_slab],
             dst_ref=recv1.at[me],
             send_sem=a2a_send.at[0],
             recv_sem=a2a_recv.at[0],
-            device_id=(other // slabs, lax.rem(other, slabs)),
+            device_id=(its_region, its_slab),
             device_id_type=MESH,
         ).start()
+
+    each_other(send_coefficients)
+
+    load_b.wait()
+    load_u.wait()
+
+    def axial_copy(field, at, up):
+        return pltpu.make_async_remote_copy(
+            src_ref=field.at[:, pl.ds(axial if up else 1, 1), cells, :],
+            dst_ref=field.at[:, pl.ds(0 if up else axial + 1, 1), cells, :],
+            send_sem=ax_send.at[at],
+            recv_sem=ax_recv.at[at],
+            device_id=(region, slab + 1 if up else slab - 1),
+            device_id_type=MESH,
+        )
+
+    up_copies = [axial_copy(b_s, 0, True), axial_copy(u_s, 1, True)]
+    down_copies = [axial_copy(b_s, 2, False), axial_copy(u_s, 3, False)]
+
+    @pl.when(slab < slabs - 1)
+    def _():
+        for copy in up_copies:
+            copy.start()
+
+    @pl.when(slab > 0)
+    def _():
+        for copy in down_copies:
+            copy.start()
+
+    lane = iota((radial, LANES), 1)
+    pair = lax.rem(lane + 1, LANES) // 2
+
+    def pack(z, totals):
+        totals = list(totals)
+        for f, field in enumerate((b_s, u_s)):
+            for c in range(3):
+                at = c * axial + z
+                plane = field[c, z + 1, PAD : PAD + radial, :]
+                totals[f] = jnp.where(pair == at, pltpu.roll(plane, 2 * at, 1), totals[f])
+                field[c, z + 1, PAD - 1 : PAD, :] = plane[0:1]
+                field[c, z + 1, PAD + radial : PAD + radial + 1, :] = plane[radial - 1 : radial]
+        return tuple(totals)
+
+    nothing = jnp.zeros((radial, LANES), F32)
+    pack_s[0], pack_s[1] = lax.fori_loop(0, axial, pack, (nothing, nothing), unroll=2)
+
+    left = lax.rem(region + regions - 1, regions)
+    right = lax.rem(region + 1, regions)
+
+    def azimuth_copy(at, target):
+        return pltpu.make_async_remote_copy(
+            src_ref=pack_s,
+            dst_ref=around_s.at[at],
+            send_sem=az_send.at[at],
+            recv_sem=az_recv.at[at],
+            device_id=(target, slab),
+            device_id_type=MESH,
+        )
+
+    azimuth_copies = [azimuth_copy(0, right)]
+    if regions > 2:
+        azimuth_copies.append(azimuth_copy(1, left))
+    for copy in azimuth_copies:
+        copy.start()
 
     single = (mode == 0.0) | (mode == azimuth_total - 1.0)
     weight_hi[...], weight_lo[...] = split(table * (jnp.where(single, 1.0, 2.0) / azimuth_total))
@@ -188,65 +260,6 @@
     radial_s[1] = kp
     radial_s[2] = inverse * (TIME_STEP * DIFFUSIVITY / (2.0 * RADIAL_STEP))
     radial_s[3] = (1.0 - 2.0 * kr - 2.0 * kz) - 2.0 * kp
-
-    load_u.wait()
-
-    def axial_copy(field, at, up):
-        return pltpu.make_async_remote_copy(
-            src_ref=field.at[:, pl.ds(axial if up else 1, 1), cells, :],
-            dst_ref=field.at[:, pl.ds(0 if up else axial + 1, 1), cells, :],
-            send_sem=ax_send.at[at],
-            recv_sem=ax_recv.at[at],
-            device_id=(region, slab + 1 if up else slab - 1),
-            device_id_type=MESH,
-        )
-
-    up_copies = [axial_copy(b_s, 0, True), axial_copy(u_s, 1, True)]
-    down_copies = [axial_copy(b_s, 2, False), axial_copy(u_s, 3, False)]
-
-    lane = iota((radial, LANES), 1)
-    pair = lax.rem(lane + 1, LANES) // 2
-
-    for f, field in enumerate((b_s, u_s)):
-        def pack(z, total, field=field):
-            for c in range(3):
-                at = c * axial + z
-                plane = field[c, z + 1, PAD : PAD + radial, :]
-                total = jnp.where(pair == at, pltpu.roll(plane, 2 * at, 1), total)
-                field[c, z + 1, PAD - 1 : PAD, :] = plane[0:1]
-                field[c, z + 1, PAD + radial : PAD + radial + 1, :] = plane[radial - 1 : radial]
-            return total
-
-        pack_s[f] = lax.fori_loop(0, axial, pack, jnp.zeros((radial, LANES), F32))
-
-    left = lax.rem(region + regions - 1, regions)
-    right = lax.rem(region + 1, regions)
-
-    def azimuth_copy(at, target):
-        return pltpu.make_async_remote_copy(
-            src_ref=pack_s,
-            dst_ref=around_s.at[at],
-            send_sem=az_send.at[at],
-            recv_sem=az_recv.at[at],
-            device_id=(target, slab),
-            device_id_type=MESH,
-        )
-
-    azimuth_copies = [azimuth_copy(0, right)]
-    if regions > 2:
-        azimuth_copies.append(azimuth_copy(1, left))
-    for copy in azimuth_copies:
-        copy.start()
-
-    @pl.when(slab < slabs - 1)
-    def _():
-        for copy in up_copies:
-            copy.start()
-
-    @pl.when(slab > 0)
-    def _():
-        for copy in down_copies:
-            copy.start()
 
     @pl.when(slab == 0)
     def _():
@@ -298,18 +311,17 @@
             send2[j, r : r + 1, :] = message[j : j + 1]
     recv2[pl.ds(me, 1)] = send2[pl.ds(slab, 1)]
 
-    @pl.loop(1, count)
-    def _(i):
-        other = lax.rem(me + i, count)
-        target = lax.rem(other, slabs)
+    def send_responses(its_region, its_slab):
         pltpu.make_async_remote_copy(
-            src_ref=send2.at[target],
+            src_ref=send2.at[its_slab],
             dst_ref=recv2.at[me],
             send_sem=a2a_send.at[1],
             recv_sem=a2a_recv.at[1],
-            device_id=(other // slabs, target),
+            device_id=(its_region, its_slab),
             device_id_type=MESH,
         ).start()
+
+    each_other(send_responses)
 
     for copy in azimuth_copies:
         copy.wait()
@@ -378,7 +390,7 @@
                 out_s[c, z, here, :] = value
         return carry
 
-    lax.fori_loop(0, axial, advance, 0)
+    lax.fori_loop(0, axial, advance, 0, unroll=2)
     load_layers.wait()
     for z in range(axial):
         trace_s[z : z + 1, :] = u_s[0, z + 1, PAD + radial - 1 : PAD + radial, :]
@@ -461,6 +473,7 @@
                 pltpu.VMEM(wall_response.shape, F32),
                 pltpu.VMEM(wall_response.shape, BF16),
                 pltpu.VMEM(wall_response.shape, BF16),
+                pltpu.VMEM((2, axial, 8, LANES), F32),
                 pltpu.VMEM((2 * axial, LANES), F32),
                 pltpu.VMEM((LANES, per_row * LANES), BF16),
                 pltpu.VMEM((LANES, per_row * LANES), BF16),
@@ -473,7 +486,7 @@
                 pltpu.VMEM((2, radial, LANES), F32),
                 pltpu.VMEM((2, 2, radial, LANES), F32),
                 pltpu.VMEM((2, radial, LANES), F32),
-                pltpu.SemaphoreType.DMA((5,)),
+                pltpu.SemaphoreType.DMA((6,)),
                 pltpu.SemaphoreType.DMA((2,)),
                 pltpu.SemaphoreType.DMA((2,)),
                 pltpu.SemaphoreType.DMA((4,)),

time: 20.9 us -> 19.7 us (0.943)
  the two profiles are of different devices: /device:TPU:1 before, /device:TPU:0 now
where the time goes in v3:
time: 19.7 us; the launch traced here: 19.5 us
  Pallas kernels  18.9 us (96%)
  between operations  0.64 us (3%)
    pallas_call x1, Pallas kernels, shards(): pl.pallas_call(functools.partial(step_kernel, regions, slabs), out_shape=...  17.7 us
    pallas_call x1, Pallas kernels, shards(): pl.pallas_call(finish_kernel, out_shape=(jax.ShapeDtypeStruct(magnetic.sh...  1.17 us

profile of v3, /device:TPU:0, one launch (start us, length us, event | category | flops | bytes accessed | tf_op | source)
XLA Modules:
  0.0 19.5 jit_solution(2439727151025622745)
XLA Ops:
  0.6 17.7 %wall_step.1 = (f32[3,16,64,128]{3,2,1,0:T(8,128)S(1)}, f32[64,128]{1,0:T(8,128)S(1)}, bf16[64,512]{1,0:T(8,128)(2,1)S(1)}, bf16[64,512]{1,0:T(8,128)(2,1)S(1)}, f32[16,128]{1,0:T(8,128)S(1)}) custom-call(s32[1,256]{1,0:T(1,128)} %bitcast.3, s32[1,128]{1,0:T(1,128)} %bitcast.4, f32[3,16,64,128]{3,2,1,0:T(8,128)} %mag_hbm.1, f32[3,16,64,128]{3,2,1,0:T(8,128)} %vel_hbm.1, ...), custom_call_target="tpu_custom_call" | custom-call | tf_op jit(solution)/shard_map/wall_step/pallas_call | solution.py:457
  18.4 1.2 %wall_finish.1 = (f32[3,16,64,128]{3,2,1,0:T(8,128)}, f32[32,128]{1,0:T(8,128)}) custom-call(f32[3,16,64,128]{3,2,1,0:T(8,128)S(1)} %get-tuple-element.9.out_ref, f32[64,128]{1,0:T(8,128)S(1)} %get-tuple-element.10.row_ref, bf16[64,512]{1,0:T(8,128)(2,1)S(1)} %get-tuple-element.11.weight_hi, bf16[64,512]{1,0:T(8,128)(2,1)S(1)} %get-tuple-element.12.weight_lo, ...), custom_call_target="tpu_custom_call" | custom-call | tf_op jit(solution)/shard_map/wall_finish/pallas_call | solution.py:513

commit v4 on v3

--- a/solution.py
+++ b/solution.py
@@ -125,6 +125,20 @@
 
     each_other(greet)
 
+    shape = (radial, LANES)
+    radius = 1.0 - (radial - iota(shape, 0).astype(F32) - 0.5) * RADIAL_STEP
+    inverse = 1.0 / radius
+    angle_step = 2.0 * math.pi / azimuth_total
+    kr = TIME_STEP * DIFFUSIVITY / RADIAL_STEP**2
+    kz = TIME_STEP * DIFFUSIVITY / AXIAL_STEP**2
+    ar = TIME_STEP / (2.0 * RADIAL_STEP)
+    az = TIME_STEP / (2.0 * AXIAL_STEP)
+    kp = inverse * inverse * (TIME_STEP * DIFFUSIVITY / angle_step**2)
+    radial_s[0] = inverse * (TIME_STEP / (2.0 * angle_step))
+    radial_s[1] = kp
+    radial_s[2] = inverse * (TIME_STEP * DIFFUSIVITY / (2.0 * RADIAL_STEP))
+    radial_s[3] = (1.0 - 2.0 * kr - 2.0 * kz) - 2.0 * kp
+
     block_hi[...] = jnp.zeros(block_hi.shape, BF16)
     block_lo[...] = jnp.zeros(block_lo.shape, BF16)
     shape = (azimuth_total, per_row * LANES)
@@ -247,20 +261,6 @@
     single = (mode == 0.0) | (mode == azimuth_total - 1.0)
     weight_hi[...], weight_lo[...] = split(table * (jnp.where(single, 1.0, 2.0) / azimuth_total))
 
-    shape = (radial, LANES)
-    radius = 1.0 - (radial - iota(shape, 0).astype(F32) - 0.5) * RADIAL_STEP
-    inverse = 1.0 / radius
-    angle_step = 2.0 * math.pi / azimuth_total
-    kr = TIME_STEP * DIFFUSIVITY / RADIAL_STEP**2
-    kz = TIME_STEP * DIFFUSIVITY / AXIAL_STEP**2
-    ar = TIME_STEP / (2.0 * RADIAL_STEP)
-    az = TIME_STEP / (2.0 * AXIAL_STEP)
-    kp = inverse * inverse * (TIME_STEP * DIFFUSIVITY / angle_step**2)
-    radial_s[0] = inverse * (TIME_STEP / (2.0 * angle_step))
-    radial_s[1] = kp
-    radial_s[2] = inverse * (TIME_STEP * DIFFUSIVITY / (2.0 * RADIAL_STEP))
-    radial_s[3] = (1.0 - 2.0 * kr - 2.0 * kz) - 2.0 * kp
-
     @pl.when(slab == 0)
     def _():
         for field in (b_s, u_s):
@@ -272,8 +272,14 @@
             field[:, axial + 1, PAD : PAD + radial, :] = jnp.zeros((3, radial, LANES), F32)
 
     load_w.wait()
-    for s in range(mode_count):
-        whi_s[s], wlo_s[s] = split(wall_s[s])
+
+    @pl.loop(0, mode_count)
+    def _(s):
+        hi, lo = split(wall_s[s])
+        at = pl.ds(pl.multiple_of(s * nz, nz), nz)
+        whi_s[at, :] = hi
+        wlo_s[at, :] = lo
+
 
     def wait_all(buffer, sem):
         part = buffer.at[pl.ds(0, count - 1)]
@@ -288,24 +294,27 @@
             got = got + recv1[g * slabs + j]
         for r in range(rows_each):
             hi, lo = split(jnp.where(own_cell, got[r : r + 1], 0.0))
-            spread_s[r, 0, axial * j : axial * (j + 1), :] = hi
-            spread_s[r, 1, axial * j : axial * (j + 1), :] = lo
+            at = 2 * nz * r + axial * j
+            spread_s[at : at + axial, :] = hi
+            spread_s[at + nz : at + nz + axial, :] = lo
     shape = (LANES, LANES)
     group = jnp.where(iota(shape, 0) // axial == iota(shape, 1) // axial, 1.0, 0.0).astype(BF16)
     shape = (nz, LANES)
     own_lane = lax.rem(iota(shape, 1), axial) == lax.rem(iota(shape, 0), axial)
     lane_group = iota(shape, 1) // (2 * axial)
+    repeated = jnp.dot(spread_s[...], group, preferred_element_type=F32).astype(BF16)
     for r in range(rows_each):
-        hi = jnp.dot(spread_s[r, 0], group, preferred_element_type=F32).astype(BF16)
-        lo = jnp.dot(spread_s[r, 1], group, preferred_element_type=F32).astype(BF16)
+        hi = repeated[2 * nz * r : 2 * nz * r + nz]
+        lo = repeated[2 * nz * r + nz : 2 * nz * (r + 1)]
         both = jnp.concatenate([hi, lo], axis=1)
+        slots = slice(nz * per_row * r, nz * per_row * (r + 1))
+        first = jnp.dot(whi_s[slots, :], both, preferred_element_type=F32)
+        second = jnp.dot(wlo_s[slots, :], hi, preferred_element_type=F32)
+        answer = first[:, :LANES] + (first[:, LANES:] + second)
         total = jnp.zeros((nz, LANES), F32)
         for q in range(per_row):
-            s = r * per_row + q
-            first = jnp.dot(whi_s[s], both, preferred_element_type=F32)
-            second = jnp.dot(wlo_s[s], hi, preferred_element_type=F32)
-            answer = first[:, :LANES] + (first[:, LANES:] + second)
-            total = jnp.where(own_lane & (lane_group == q), answer, total)
+            part = answer[nz * q : nz * (q + 1)]
+            total = jnp.where(own_lane & (lane_group == q), part, total)
         message = jnp.sum(total.reshape(slabs, axial, LANES), axis=1)
         for j in range(slabs):
             send2[j, r : r + 1, :] = message[j : j + 1]
@@ -471,14 +480,14 @@
                 pltpu.VMEM((1, azimuth_total), jnp.int32),
                 pltpu.VMEM((1, azimuth), jnp.int32),
                 pltpu.VMEM(wall_response.shape, F32),
-                pltpu.VMEM(wall_response.shape, BF16),
-                pltpu.VMEM(wall_response.shape, BF16),
+                pltpu.VMEM((mode_count * nz, nz), BF16),
+                pltpu.VMEM((mode_count * nz, nz), BF16),
                 pltpu.VMEM((2, axial, 8, LANES), F32),
                 pltpu.VMEM((2 * axial, LANES), F32),
                 pltpu.VMEM((LANES, per_row * LANES), BF16),
                 pltpu.VMEM((LANES, per_row * LANES), BF16),
                 pltpu.VMEM((4, radial, LANES), F32),
-                pltpu.VMEM((rows_each, 2, nz, LANES), BF16),
+                pltpu.VMEM((rows_each * 2 * nz, LANES), BF16),
                 pltpu.VMEM((count, rows_each, LANES), F32),
                 pltpu.VMEM((count, rows_each, LANES), F32),
                 pltpu.VMEM((slabs, rows_each, LANES), F32),

time: 19.7 us -> 19.5 us (0.990)
  Pallas kernels: 18.9 us -> 18.7 us
    pallas_call x1, Pallas kernels: 17.7 us -> 17.5 us  [shards(): pl.pallas_call(functools.partial(step_kernel, regions, slabs), out_shape=...]
where the time goes in v4:
time: 19.5 us; the launch traced here: 19.3 us
  Pallas kernels  18.7 us (96%)
  between operations  0.64 us (3%)
    pallas_call x1, Pallas kernels, shards(): pl.pallas_call(functools.partial(step_kernel, regions, slabs), out_shape=...  17.5 us
    pallas_call x1, Pallas kernels, shards(): pl.pallas_call(finish_kernel, out_shape=(jax.ShapeDtypeStruct(magnetic.sh...  1.17 us

profile of v4, /device:TPU:0, one launch (start us, length us, event | category | flops | bytes accessed | tf_op | source)
XLA Modules:
  0.0 19.3 jit_solution(5696898799065573169)
XLA Ops:
  0.6 17.5 %wall_step.1 = (f32[3,16,64,128]{3,2,1,0:T(8,128)S(1)}, f32[64,128]{1,0:T(8,128)S(1)}, bf16[64,512]{1,0:T(8,128)(2,1)S(1)}, bf16[64,512]{1,0:T(8,128)(2,1)S(1)}, f32[16,128]{1,0:T(8,128)S(1)}) custom-call(s32[1,256]{1,0:T(1,128)} %bitcast.3, s32[1,128]{1,0:T(1,128)} %bitcast.4, f32[3,16,64,128]{3,2,1,0:T(8,128)} %mag_hbm.1, f32[3,16,64,128]{3,2,1,0:T(8,128)} %vel_hbm.1, ...), custom_call_target="tpu_custom_call" | custom-call | tf_op jit(solution)/shard_map/wall_step/pallas_call | solution.py:466
  18.2 1.2 %wall_finish.1 = (f32[3,16,64,128]{3,2,1,0:T(8,128)}, f32[32,128]{1,0:T(8,128)}) custom-call(f32[3,16,64,128]{3,2,1,0:T(8,128)S(1)} %get-tuple-element.9.out_ref, f32[64,128]{1,0:T(8,128)S(1)} %get-tuple-element.10.row_ref, bf16[64,512]{1,0:T(8,128)(2,1)S(1)} %get-tuple-element.11.weight_hi, bf16[64,512]{1,0:T(8,128)(2,1)S(1)} %get-tuple-element.12.weight_lo, ...), custom_call_target="tpu_custom_call" | custom-call | tf_op jit(solution)/shard_map/wall_finish/pallas_call | solution.py:522

commit v5 on v4

--- a/solution.py
+++ b/solution.py
@@ -23,6 +23,16 @@
 
 def iota(shape, dim):
     return lax.broadcasted_iota(jnp.int32, shape, dim)
+
+
+def high(x, n):
+    if n & (n - 1):
+        return x // n
+    return lax.shift_right_logical(x, jnp.full(x.shape, n.bit_length() - 1, x.dtype))
+
+
+def low(x, n):
+    return lax.rem(x, n) if n & (n - 1) else x & (n - 1)
 
 
 def split(x):
@@ -142,9 +152,9 @@
     block_hi[...] = jnp.zeros(block_hi.shape, BF16)
     block_lo[...] = jnp.zeros(block_lo.shape, BF16)
     shape = (azimuth_total, per_row * LANES)
-    picks = jnp.where(lax.rem(iota(shape, 0), per_row) == iota(shape, 1) // LANES, 1.0, 0.0)
+    picks = jnp.where(low(iota(shape, 0), per_row) == high(iota(shape, 1), LANES), 1.0, 0.0)
     shape = (slot_rows, azimuth_total)
-    mine = iota(shape, 1) // per_row == iota(shape, 0)
+    mine = high(iota(shape, 1), per_row) == iota(shape, 0)
     load_modes.wait()
     modes = mode_s[...].astype(F32)
     tens = jnp.floor(modes * (1.0 / 32.0))
@@ -157,7 +167,7 @@
     mode = 32.0 * parts[:slot_rows] + parts[slot_rows:]
     half = jnp.floor(mode * 0.5)
     odd = mode - 2.0 * half
-    cell = region * LANES + lax.rem(iota(mode.shape, 1), LANES)
+    cell = region * LANES + low(iota(mode.shape, 1), LANES)
     turn = (half + odd) * (2 * cell + 1).astype(F32) - odd * (azimuth_total // 2)
     turn = turn * (0.5 / azimuth_total)
     turn = turn - jnp.floor(turn + 0.5)
@@ -223,7 +233,7 @@
             copy.start()
 
     lane = iota((radial, LANES), 1)
-    pair = lax.rem(lane + 1, LANES) // 2
+    pair = high(low(lane + 1, LANES), 2)
 
     def pack(z, totals):
         totals = list(totals)
@@ -287,7 +297,7 @@
 
     wait_all(recv1, a2a_recv.at[0])
     shape = (axial, LANES)
-    own_cell = lax.rem(iota(shape, 1), axial) == iota(shape, 0)
+    own_cell = low(iota(shape, 1), axial) == iota(shape, 0)
     for j in range(slabs):
         got = recv1[j]
         for g in range(1, regions):
@@ -298,10 +308,10 @@
             spread_s[at : at + axial, :] = hi
             spread_s[at + nz : at + nz + axial, :] = lo
     shape = (LANES, LANES)
-    group = jnp.where(iota(shape, 0) // axial == iota(shape, 1) // axial, 1.0, 0.0).astype(BF16)
+    group = jnp.where(high(iota(shape, 0), axial) == high(iota(shape, 1), axial), 1.0, 0.0).astype(BF16)
     shape = (nz, LANES)
-    own_lane = lax.rem(iota(shape, 1), axial) == lax.rem(iota(shape, 0), axial)
-    lane_group = iota(shape, 1) // (2 * axial)
+    own_lane = low(iota(shape, 1), axial) == low(iota(shape, 0), axial)
+    lane_group = high(iota(shape, 1), 2 * axial)
     repeated = jnp.dot(spread_s[...], group, preferred_element_type=F32).astype(BF16)
     for r in range(rows_each):
         hi = repeated[2 * nz * r : 2 * nz * r + nz]
@@ -335,7 +345,7 @@
     for copy in azimuth_copies:
         copy.wait()
 
-    even = lax.rem(lane, 2) == 0
+    even = low(lane, 2) == 0
     for f in range(2):
         from_left = around_s[0, f]
         from_right = around_s[len(azimuth_copies) - 1, f]
@@ -358,14 +368,15 @@
             copy.wait_recv()
 
     depth = 16
+    first_row = PAD + slab // slabs
     first_lane = iota((depth, LANES), 1) == 0
     last_lane = iota((depth, LANES), 1) == LANES - 1
 
     def advance(z, carry):
         for start in range(0, radial, depth):
             rows = slice(PAD + start, PAD + start + depth)
-            above = slice(PAD + start + 1, PAD + start + depth + 1)
-            below = slice(PAD + start - 1, PAD + start + depth - 1)
+            above = pl.ds(first_row + (start + 1), depth)
+            below = pl.ds(first_row + (start - 1), depth)
             here = slice(start, start + depth)
             ap = radial_s[0, here, :]
             kp = radial_s[1, here, :]
@@ -373,7 +384,7 @@
             kc = radial_s[3, here, :]
 
             def around(f, c, center):
-                shift = lax.rem(LANES - lax.rem(2 * (c * axial + z), LANES), LANES)
+                shift = low(LANES - 2 * (c * axial + z), LANES)
                 halo = pltpu.roll(halo_s[f, here, :], shift, 1)
                 before = jnp.where(first_lane, halo, pltpu.roll(center, 1, 1))
                 after = jnp.where(last_lane, halo, pltpu.roll(center, LANES - 1, 1))

time: 19.5 us -> 19.5 us (level)
  no operation moved by 1% of the time
where the time goes in v5:
time: 19.5 us; the launch traced here: 19.3 us
  Pallas kernels  18.7 us (96%)
  between operations  0.64 us (3%)
    pallas_call x1, Pallas kernels, shards(): pl.pallas_call(functools.partial(step_kernel, regions, slabs), out_shape=...  17.5 us
    pallas_call x1, Pallas kernels, shards(): pl.pallas_call(finish_kernel, out_shape=(jax.ShapeDtypeStruct(magnetic.sh...  1.17 us

profile of v5, /device:TPU:0, one launch (start us, length us, event | category | flops | bytes accessed | tf_op | source)
XLA Modules:
  0.0 19.3 jit_solution(13549992452057429554)
XLA Ops:
  0.6 17.5 %wall_step.1 = (f32[3,16,64,128]{3,2,1,0:T(8,128)S(1)}, f32[64,128]{1,0:T(8,128)S(1)}, bf16[64,512]{1,0:T(8,128)(2,1)S(1)}, bf16[64,512]{1,0:T(8,128)(2,1)S(1)}, f32[16,128]{1,0:T(8,128)S(1)}) custom-call(s32[1,256]{1,0:T(1,128)} %bitcast.3, s32[1,128]{1,0:T(1,128)} %bitcast.4, f32[3,16,64,128]{3,2,1,0:T(8,128)} %mag_hbm.1, f32[3,16,64,128]{3,2,1,0:T(8,128)} %vel_hbm.1, ...), custom_call_target="tpu_custom_call" | custom-call | tf_op jit(solution)/shard_map/wall_step/pallas_call | solution.py:477
  18.2 1.2 %wall_finish.1 = (f32[3,16,64,128]{3,2,1,0:T(8,128)}, f32[32,128]{1,0:T(8,128)}) custom-call(f32[3,16,64,128]{3,2,1,0:T(8,128)S(1)} %get-tuple-element.9.out_ref, f32[64,128]{1,0:T(8,128)S(1)} %get-tuple-element.10.row_ref, bf16[64,512]{1,0:T(8,128)(2,1)S(1)} %get-tuple-element.11.weight_hi, bf16[64,512]{1,0:T(8,128)(2,1)S(1)} %get-tuple-element.12.weight_lo, ...), custom_call_target="tpu_custom_call" | custom-call | tf_op jit(solution)/shard_map/wall_finish/pallas_call | solution.py:533

commit v6 on v5

--- a/solution.py
+++ b/solution.py
@@ -295,6 +295,64 @@
         part = buffer.at[pl.ds(0, count - 1)]
         pltpu.make_async_copy(part, part, sem).wait()
 
+    for copy in azimuth_copies:
+        copy.wait()
+
+    even = low(lane, 2) == 0
+    for f in range(2):
+        from_left = around_s[0, f]
+        from_right = around_s[len(azimuth_copies) - 1, f]
+        halo_s[f] = jnp.where(
+            even, pltpu.roll(from_left, 1, 1), pltpu.roll(from_right, LANES - 1, 1)
+        )
+
+    depth = 16
+    first_row = PAD + slab // slabs
+    first_lane = iota((depth, LANES), 1) == 0
+    last_lane = iota((depth, LANES), 1) == LANES - 1
+
+    def advance(turn, carry):
+        z = lax.rem(turn, axial)
+        for start in range(0, radial, depth):
+            rows = slice(PAD + start, PAD + start + depth)
+            above = pl.ds(first_row + (start + 1), depth)
+            below = pl.ds(first_row + (start - 1), depth)
+            here = slice(start, start + depth)
+            ap = radial_s[0, here, :]
+            kp = radial_s[1, here, :]
+            k1 = radial_s[2, here, :]
+            kc = radial_s[3, here, :]
+
+            def around(f, c, center):
+                shift = low(LANES - 2 * (c * axial + z), LANES)
+                halo = pltpu.roll(halo_s[f, here, :], shift, 1)
+                before = jnp.where(first_lane, halo, pltpu.roll(center, 1, 1))
+                after = jnp.where(last_lane, halo, pltpu.roll(center, LANES - 1, 1))
+                return before, after
+
+            b = [b_s[c, z + 1, rows, :] for c in range(3)]
+            u = [u_s[c, z + 1, rows, :] for c in range(3)]
+            ur, up, uz = ar * u[0] - k1, ap * u[1], az * u[2]
+            br, bp, bz = ar * b[0], ap * b[1], az * b[2]
+            r_next, r_last = kr - ur, kr + ur
+            p_next, p_last = kp - up, kp + up
+            z_next, z_last = kz - uz, kz + uz
+            for c in range(3):
+                before, after = around(0, c, b[c])
+                value = b[c] * kc
+                value += r_next * b_s[c, z + 1, above, :] + r_last * b_s[c, z + 1, below, :]
+                value += p_next * after + p_last * before
+                value += z_next * b_s[c, z + 2, rows, :] + z_last * b_s[c, z, rows, :]
+                before, after = around(1, c, u[c])
+                value += br * (u_s[c, z + 1, above, :] - u_s[c, z + 1, below, :])
+                value += bp * (after - before)
+                value += bz * (u_s[c, z + 2, rows, :] - u_s[c, z, rows, :])
+                out_s[c, z, here, :] = value
+        return carry
+
+    early = 3 * axial // 8
+    lax.fori_loop(1, 1 + early, advance, 0, unroll=2)
+
     wait_all(recv1, a2a_recv.at[0])
     shape = (axial, LANES)
     own_cell = low(iota(shape, 1), axial) == iota(shape, 0)
@@ -342,17 +400,6 @@
 
     each_other(send_responses)
 
-    for copy in azimuth_copies:
-        copy.wait()
-
-    even = low(lane, 2) == 0
-    for f in range(2):
-        from_left = around_s[0, f]
-        from_right = around_s[len(azimuth_copies) - 1, f]
-        halo_s[f] = jnp.where(
-            even, pltpu.roll(from_left, 1, 1), pltpu.roll(from_right, LANES - 1, 1)
-        )
-
     @pl.when(slab < slabs - 1)
     def _():
         for copy in up_copies:
@@ -367,50 +414,7 @@
         for copy in up_copies:
             copy.wait_recv()
 
-    depth = 16
-    first_row = PAD + slab // slabs
-    first_lane = iota((depth, LANES), 1) == 0
-    last_lane = iota((depth, LANES), 1) == LANES - 1
-
-    def advance(z, carry):
-        for start in range(0, radial, depth):
-            rows = slice(PAD + start, PAD + start + depth)
-            above = pl.ds(first_row + (start + 1), depth)
-            below = pl.ds(first_row + (start - 1), depth)
-            here = slice(start, start + depth)
-            ap = radial_s[0, here, :]
-            kp = radial_s[1, here, :]
-            k1 = radial_s[2, here, :]
-            kc = radial_s[3, here, :]
-
-            def around(f, c, center):
-                shift = low(LANES - 2 * (c * axial + z), LANES)
-                halo = pltpu.roll(halo_s[f, here, :], shift, 1)
-                before = jnp.where(first_lane, halo, pltpu.roll(center, 1, 1))
-                after = jnp.where(last_lane, halo, pltpu.roll(center, LANES - 1, 1))
-                return before, after
-
-            b = [b_s[c, z + 1, rows, :] for c in range(3)]
-            u = [u_s[c, z + 1, rows, :] for c in range(3)]
-            ur, up, uz = ar * u[0] - k1, ap * u[1], az * u[2]
-            br, bp, bz = ar * b[0], ap * b[1], az * b[2]
-            r_next, r_last = kr - ur, kr + ur
-            p_next, p_last = kp - up, kp + up
-            z_next, z_last = kz - uz, kz + uz
-            for c in range(3):
-                before, after = around(0, c, b[c])
-                value = b[c] * kc
-                value += r_next * b_s[c, z + 1, above, :] + r_last * b_s[c, z + 1, below, :]
-                value += p_next * after + p_last * before
-                value += z_next * b_s[c, z + 2, rows, :] + z_last * b_s[c, z, rows, :]
-                before, after = around(1, c, u[c])
-                value += br * (u_s[c, z + 1, above, :] - u_s[c, z + 1, below, :])
-                value += bp * (after - before)
-                value += bz * (u_s[c, z + 2, rows, :] - u_s[c, z, rows, :])
-                out_s[c, z, here, :] = value
-        return carry
-
-    lax.fori_loop(0, axial, advance, 0, unroll=2)
+    lax.fori_loop(1 + early, axial + 1, advance, 0, unroll=2)
     load_layers.wait()
     for z in range(axial):
         trace_s[z : z + 1, :] = u_s[0, z + 1, PAD + radial - 1 : PAD + radial, :]

time: 19.5 us -> 19.7 us (1.010)
  Pallas kernels: 18.7 us -> 18.9 us
where the time goes in v6:
time: 19.7 us; the launch traced here: 19.5 us
  Pallas kernels  18.9 us (96%)
  between operations  0.64 us (3%)
    pallas_call x1, Pallas kernels, shards(): pl.pallas_call(functools.partial(step_kernel, regions, slabs), out_shape=...  17.7 us
    pallas_call x1, Pallas kernels, shards(): pl.pallas_call(finish_kernel, out_shape=(jax.ShapeDtypeStruct(magnetic.sh...  1.17 us

profile of v6, /device:TPU:0, one launch (start us, length us, event | category | flops | bytes accessed | tf_op | source)
XLA Modules:
  0.0 19.5 jit_solution(10321642522837830470)
XLA Ops:
  0.6 17.7 %wall_step.1 = (f32[3,16,64,128]{3,2,1,0:T(8,128)S(1)}, f32[64,128]{1,0:T(8,128)S(1)}, bf16[64,512]{1,0:T(8,128)(2,1)S(1)}, bf16[64,512]{1,0:T(8,128)(2,1)S(1)}, f32[16,128]{1,0:T(8,128)S(1)}) custom-call(s32[1,256]{1,0:T(1,128)} %bitcast.3, s32[1,128]{1,0:T(1,128)} %bitcast.4, f32[3,16,64,128]{3,2,1,0:T(8,128)} %mag_hbm.1, f32[3,16,64,128]{3,2,1,0:T(8,128)} %vel_hbm.1, ...), custom_call_target="tpu_custom_call" | custom-call | tf_op jit(solution)/shard_map/wall_step/pallas_call | solution.py:481
  18.3 1.2 %wall_finish.1 = (f32[3,16,64,128]{3,2,1,0:T(8,128)}, f32[32,128]{1,0:T(8,128)}) custom-call(f32[3,16,64,128]{3,2,1,0:T(8,128)S(1)} %get-tuple-element.9.out_ref, f32[64,128]{1,0:T(8,128)S(1)} %get-tuple-element.10.row_ref, bf16[64,512]{1,0:T(8,128)(2,1)S(1)} %get-tuple-element.11.weight_hi, bf16[64,512]{1,0:T(8,128)(2,1)S(1)} %get-tuple-element.12.weight_lo, ...), custom_call_target="tpu_custom_call" | custom-call | tf_op jit(solution)/shard_map/wall_finish/pallas_call | solution.py:537

commit v7 on v6

--- a/solution.py
+++ b/solution.py
@@ -222,16 +222,6 @@
     up_copies = [axial_copy(b_s, 0, True), axial_copy(u_s, 1, True)]
     down_copies = [axial_copy(b_s, 2, False), axial_copy(u_s, 3, False)]
 
-    @pl.when(slab < slabs - 1)
-    def _():
-        for copy in up_copies:
-            copy.start()
-
-    @pl.when(slab > 0)
-    def _():
-        for copy in down_copies:
-            copy.start()
-
     lane = iota((radial, LANES), 1)
     pair = high(low(lane + 1, LANES), 2)
 
@@ -267,6 +257,16 @@
         azimuth_copies.append(azimuth_copy(1, left))
     for copy in azimuth_copies:
         copy.start()
+
+    @pl.when(slab < slabs - 1)
+    def _():
+        for copy in up_copies:
+            copy.start()
+
+    @pl.when(slab > 0)
+    def _():
+        for copy in down_copies:
+            copy.start()
 
     single = (mode == 0.0) | (mode == azimuth_total - 1.0)
     weight_hi[...], weight_lo[...] = split(table * (jnp.where(single, 1.0, 2.0) / azimuth_total))
@@ -350,7 +350,7 @@
                 out_s[c, z, here, :] = value
         return carry
 
-    early = 3 * axial // 8
+    early = axial // 8
     lax.fori_loop(1, 1 + early, advance, 0, unroll=2)
 
     wait_all(recv1, a2a_recv.at[0])
@@ -400,6 +400,8 @@
 
     each_other(send_responses)
 
+    lax.fori_loop(1 + early, axial - 1, advance, 0, unroll=2)
+
     @pl.when(slab < slabs - 1)
     def _():
         for copy in up_copies:
@@ -414,7 +416,7 @@
         for copy in up_copies:
             copy.wait_recv()
 
-    lax.fori_loop(1 + early, axial + 1, advance, 0, unroll=2)
+    lax.fori_loop(axial - 1, axial + 1, advance, 0, unroll=2)
     load_layers.wait()
     for z in range(axial):
         trace_s[z : z + 1, :] = u_s[0, z + 1, PAD + radial - 1 : PAD + radial, :]

time: 19.7 us -> 19.5 us (0.990)
  Pallas kernels: 18.9 us -> 18.7 us
where the time goes in v7:
time: 19.5 us; the launch traced here: 19.3 us
  Pallas kernels  18.7 us (96%)
  between operations  0.64 us (3%)
    pallas_call x1, Pallas kernels, shards(): pl.pallas_call(functools.partial(step_kernel, regions, slabs), out_shape=...  17.5 us
    pallas_call x1, Pallas kernels, shards(): pl.pallas_call(finish_kernel, out_shape=(jax.ShapeDtypeStruct(magnetic.sh...  1.17 us

profile of v7, /device:TPU:0, one launch (start us, length us, event | category | flops | bytes accessed | tf_op | source)
XLA Modules:
  0.0 19.3 jit_solution(13080346349160597257)
XLA Ops:
  0.6 17.5 %wall_step.1 = (f32[3,16,64,128]{3,2,1,0:T(8,128)S(1)}, f32[64,128]{1,0:T(8,128)S(1)}, bf16[64,512]{1,0:T(8,128)(2,1)S(1)}, bf16[64,512]{1,0:T(8,128)(2,1)S(1)}, f32[16,128]{1,0:T(8,128)S(1)}) custom-call(s32[1,256]{1,0:T(1,128)} %bitcast.3, s32[1,128]{1,0:T(1,128)} %bitcast.4, f32[3,16,64,128]{3,2,1,0:T(8,128)} %mag_hbm.1, f32[3,16,64,128]{3,2,1,0:T(8,128)} %vel_hbm.1, ...), custom_call_target="tpu_custom_call" | custom-call | tf_op jit(solution)/shard_map/wall_step/pallas_call | solution.py:483
  18.2 1.2 %wall_finish.1 = (f32[3,16,64,128]{3,2,1,0:T(8,128)}, f32[32,128]{1,0:T(8,128)}) custom-call(f32[3,16,64,128]{3,2,1,0:T(8,128)S(1)} %get-tuple-element.9.out_ref, f32[64,128]{1,0:T(8,128)S(1)} %get-tuple-element.10.row_ref, bf16[64,512]{1,0:T(8,128)(2,1)S(1)} %get-tuple-element.11.weight_hi, bf16[64,512]{1,0:T(8,128)(2,1)S(1)} %get-tuple-element.12.weight_lo, ...), custom_call_target="tpu_custom_call" | custom-call | tf_op jit(solution)/shard_map/wall_finish/pallas_call | solution.py:539
